TPU v7x, 128 devices: a whole 4x4x4 slice. The times are simulated.
128 devices in a mesh: band: 4 (over z_lo, core), dom: 32 (over y, z_hi, x).
Axes of the slice: x: 4, y: 4, z: 4 (z_hi: 2, z_lo: 2; z = z_hi * 2 + z_lo), core: 2. Of those that a mesh axis runs over, the one named last changes fastest.
Arguments:
- orbitals: float32 [192, 96, 2304], P('band', 'dom'), as said below
- potential: float32 [96, 2304], P('dom'), may hold values from -1 to 1
Outputs:
- rotated: float32 [192, 96, 2304], P('band', 'dom')
Inputs may be any that keep to these rules, and one draw needn't show every extreme that they name: real-valued orbitals.
All inputs are finite; a program needn't handle non-finite values.
Results may differ from a plain program's by a relative error of at most 0.00013.
Values sent between devices are 32-bit elements; how exact they have to be, the bound alone decides.
A program may use at most 192 MiB of HBM per device.

v0:
```python
import jax
import jax.numpy as jnp
from jax import lax
from jax.sharding import PartitionSpec as P

NY = 48
NZ = 48


stencil_weights = (
    -5369.0 / 1800.0,
    12.0 / 7.0,
    -15.0 / 56.0,
    10.0 / 189.0,
    -1.0 / 112.0,
    2.0 / 1925.0,
    -1.0 / 16632.0,
)
centre_shift = 7.0
half_width = 5.0


def from_behind(value, axis, by):
    peers = lax.axis_size(axis)
    return lax.ppermute(value, axis, [(i, (i + by) % peers) for i in range(peers)])


def band_matrix(row_total, column_total, offset, periodic):
    row_index = lax.broadcasted_iota(jnp.int32, (row_total, column_total), 0)
    column_index = lax.broadcasted_iota(jnp.int32, (row_total, column_total), 1)
    distance = row_index - column_index - offset
    if periodic:
        distance = jnp.mod(distance, row_total)
        distance = jnp.minimum(distance, row_total - distance)
    else:
        distance = jnp.abs(distance)
    weights = jnp.zeros((row_total, column_total), jnp.float32)
    for stride in range(7):
        weights = weights + jnp.where(
            distance == stride, jnp.float32(stencil_weights[stride]), jnp.float32(0.0)
        )
    return weights


def apply_hamiltonian(padded, potential_part):
    row_count = padded.shape[0]
    padded_width = padded.shape[1]
    inner_width = padded_width - 12
    centre = padded[:, 6 : 6 + inner_width]
    across_x = band_matrix(padded_width, inner_width, 6, False)
    across_y = band_matrix(NY, NY, 0, True)
    across_z = band_matrix(NZ, NZ, 0, True)
    along_x = jnp.einsum(
        "rpc,pq->rqc",
        padded,
        across_x,
        precision=lax.Precision.HIGHEST,
        preferred_element_type=jnp.float32,
    )
    grid = centre.reshape(row_count, inner_width, NY, NZ)
    along_y = jnp.einsum(
        "rxyz,yw->rxwz",
        grid,
        across_y,
        precision=lax.Precision.HIGHEST,
        preferred_element_type=jnp.float32,
    )
    along_z = jnp.einsum(
        "rxyz,zw->rxyw",
        grid,
        across_z,
        precision=lax.Precision.HIGHEST,
        preferred_element_type=jnp.float32,
    )
    sideways = (along_y + along_z).reshape(row_count, inner_width, NY * NZ)
    return -0.5 * (along_x + sideways) + potential_part * centre


def chebyshev_step(padded, potential_part, previous):
    centre = padded[:, 6 : padded.shape[1] - 6]
    applied = apply_hamiltonian(padded, potential_part)
    if previous is None:
        return (applied - centre_shift * centre) / half_width
    return 2.0 * (applied - centre_shift * centre) / half_width - previous


def shift_offsets(plane_count, width):
    reach = -(-width // plane_count)
    return list(range(reach, 0, -1)) + list(range(-1, -reach - 1, -1))


def assemble(field, pieces):
    reach = len(pieces) // 2
    lower = jnp.concatenate(pieces[:reach], axis=1)
    upper = jnp.concatenate(pieces[reach:], axis=1)
    return jnp.concatenate([lower, field, upper], axis=1)


def refresh(field):
    pieces = [from_behind(field, "dom", offset) for offset in shift_offsets(field.shape[1], 6)]
    return assemble(field, pieces)


def contract(left_rows, right_rows):
    return lax.dot_general(
        left_rows,
        right_rows,
        (((1,), (1,)), ((), ())),
        precision=lax.Precision.HIGHEST,
        preferred_element_type=jnp.float32,
    )


def per_device(orbitals, potential):
    row_count = orbitals.shape[0]
    previous = orbitals
    current = chebyshev_step(refresh(orbitals), potential, None)
    for step_index in range(3):
        following = chebyshev_step(refresh(current), potential, previous)
        previous = current
        current = following
    flattened = current.reshape(row_count, -1)
    cell_count = flattened.shape[1] * lax.axis_size("dom")
    orbital_count = row_count * lax.axis_size("band")
    block_start = lax.axis_index("band") * row_count
    everyone = lax.all_gather(flattened, "band", axis=0, tiled=True)
    own_rows = contract(flattened, everyone)
    zero_index = block_start * 0
    partial_value = lax.dynamic_update_slice(
        jnp.zeros((orbital_count, orbital_count), jnp.float32), own_rows, (block_start, zero_index)
    )
    intersection = lax.psum(partial_value, ("band", "dom")) / cell_count
    lower_factor = jnp.linalg.cholesky(intersection)
    inverse = jax.scipy.linalg.solve_triangular(
        lower_factor, jnp.eye(orbital_count, dtype=jnp.float32), lower=True
    )
    own_inverse = lax.dynamic_slice_in_dim(inverse, block_start, row_count, 0)
    returned = jnp.dot(
        own_inverse, everyone, precision=lax.Precision.HIGHEST, preferred_element_type=jnp.float32
    )
    return returned.reshape(current.shape)


def solution(mesh):
    placed = (P("band", "dom", None), P("dom", None))
    return jax.shard_map(
        per_device, mesh=mesh, in_specs=placed, out_specs=P("band", "dom", None), check_vma=False
    )
```

profile of v0, /device:TPU:1, one launch (start us, length us, event | category | flops | bytes accessed | tf_op | source)
XLA Modules:
  0.0 737.4 jit_solution(2393699060330014031)
XLA Ops:
  6.5 3.6 collective-permute-start
  10.4 6.9 collective-permute-start.2
  18.0 3.3 reshape.54
  21.3 3.5 copy.118
  24.8 3.2 fusion.18
  28.0 5.0 bitcast_add_fusion.3
  33.0 4.4 reshape.100
  37.4 7.7 %collective-permute-done = f32[48,3,2304]{2,0,1:T(8,128)} collective-permute-done((f32[48,3,2304]{2,0,1:T(8,128)}, f32[48,3,2304]{2,0,1:T(8,128)}, u32[]{:S(2)}, u32[]{:S(2)}) %collective-permute-start) | collective-permute-done | bytes 1327136 | tf_op jit(solution)/shard_map/ppermute | solution.py:25
  45.1 3.5 copy.116
  48.6 26.3 %collective-permute-done.1 = f32[48,3,2304]{2,0,1:T(8,128)} collective-permute-done((f32[48,3,2304]{2,0,1:T(8,128)}, f32[48,3,2304]{2,0,1:T(8,128)}, u32[]{:S(2)}, u32[]{:S(2)}) %collective-permute-start.1) | collective-permute-done | bytes 1327136 | tf_op jit(solution)/shard_map/ppermute | solution.py:25
  74.9 3.5 copy.117
  78.4 3.5 copy.119
  81.8 17.6 %collective-permute-done.3 = f32[48,3,2304]{2,0,1:T(8,128)} collective-permute-done((f32[48,3,2304]{2,0,1:T(8,128)}, f32[48,3,2304]{2,0,1:T(8,128)}, u32[]{:S(2)}, u32[]{:S(2)}) %collective-permute-start.3) | collective-permute-done | bytes 1327136 | tf_op jit(solution)/shard_map/ppermute | solution.py:25
  99.4 3.5 copy.120
  102.9 50.7 %concatenate.21 = f32[48,15,2304]{2,1,0:T(8,128)} concatenate(f32[48,3,2304]{2,1,0:T(4,128)} %copy.116, f32[48,3,2304]{2,1,0:T(4,128)} %copy.117, f32[48,3,2304]{2,1,0:T(4,128)S(1)} %copy-done.8, f32[48,3,2304]{2,1,0:T(4,128)} %copy.119, f32[48,3,2304]{2,1,0:T(4,128)} %copy.120), dimensions={1} | concatenate | bytes 13271040 | tf_op jit(solution)/shard_map/concatenate | solution.py:96
  153.6 5.7 fusion.82
  159.4 2.1 broadcast_multiply_fusion
  161.5 2.8 collective-permute-start.4
  165.2 6.9 collective-permute-start.6
  172.1 3.7 reshape.56
  175.8 3.0 fusion.14
  178.8 5.0 bitcast_add_fusion.2
  183.8 5.2 reshape.101
  189.0 7.9 %collective-permute-done.4 = f32[48,3,2304]{2,0,1:T(8,128)} collective-permute-done((f32[48,3,2304]{2,0,1:T(8,128)}, f32[48,3,2304]{2,0,1:T(8,128)}, u32[]{:S(2)}, u32[]{:S(2)}) %collective-permute-start.4) | collective-permute-done | bytes 1327136 | tf_op jit(solution)/shard_map/ppermute | solution.py:25
  198.4 30.9 %collective-permute-done.5 = f32[48,3,2304]{2,0,1:T(8,128)} collective-permute-done((f32[48,3,2304]{2,0,1:T(8,128)}, f32[48,3,2304]{2,0,1:T(8,128)}, u32[]{:S(2)}, u32[]{:S(2)}) %collective-permute-start.5) | collective-permute-done | bytes 1327136 | tf_op jit(solution)/shard_map/ppermute | solution.py:25
  229.2 1.4 constant_dynamic-update-slice_fusion.3
  230.8 1.4 constant_dynamic-update-slice_fusion.1
  232.3 17.2 %collective-permute-done.7 = f32[48,3,2304]{2,0,1:T(8,128)} collective-permute-done((f32[48,3,2304]{2,0,1:T(8,128)}, f32[48,3,2304]{2,0,1:T(8,128)}, u32[]{:S(2)}, u32[]{:S(2)}) %collective-permute-start.7) | collective-permute-done | bytes 1327136 | tf_op jit(solution)/shard_map/ppermute | solution.py:25
  250.9 7.3 fusion.4
  258.9 2.8 collective-permute-start.8
  262.1 6.9 collective-permute-start.10
  268.9 3.6 reshape.58
  272.6 5.3 fusion.10
  277.9 5.0 bitcast_add_fusion.1
  282.9 5.4 reshape.102
  288.3 5.0 collective-permute-done.8
  294.7 32.7 %collective-permute-done.9 = f32[48,3,2304]{2,0,1:T(8,128)} collective-permute-done((f32[48,3,2304]{2,0,1:T(8,128)S(1)}, f32[48,3,2304]{2,0,1:T(8,128)}, u32[]{:S(2)}, u32[]{:S(2)}) %collective-permute-start.9) | collective-permute-done | bytes 1327136 | tf_op jit(solution)/shard_map/ppermute | solution.py:25
  327.5 1.4 constant_dynamic-update-slice_fusion.8
  329.0 1.4 constant_dynamic-update-slice_fusion.6
  330.4 18.6 %collective-permute-done.11 = f32[48,3,2304]{2,0,1:T(8,128)} collective-permute-done((f32[48,3,2304]{2,0,1:T(8,128)S(1)}, f32[48,3,2304]{2,0,1:T(8,128)}, u32[]{:S(2)}, u32[]{:S(2)}) %collective-permute-start.11) | collective-permute-done | bytes 1327136 | tf_op jit(solution)/shard_map/ppermute | solution.py:25
  350.4 7.3 fusion.2
  357.8 1.8 fusion.40
  359.6 3.0 collective-permute-start.12
  362.6 7.2 collective-permute-start.14
  369.8 4.5 reshape.60
  374.3 5.3 fusion.6
  379.6 5.0 bitcast_add_fusion
  384.6 4.4 reshape.103
  389.0 4.2 collective-permute-done.12
  394.6 34.6 %collective-permute-done.13 = f32[48,3,2304]{2,0,1:T(8,128)} collective-permute-done((f32[48,3,2304]{2,0,1:T(8,128)}, f32[48,3,2304]{2,0,1:T(8,128)}, u32[]{:S(2)}, u32[]{:S(2)}) %collective-permute-start.13) | collective-permute-done | bytes 1327136 | tf_op jit(solution)/shard_map/ppermute | solution.py:25
  429.2 1.4 constant_dynamic-update-slice_fusion.13
  430.6 1.4 constant_dynamic-update-slice_fusion.12
  432.0 1.4 constant_dynamic-update-slice_fusion.11
  433.4 12.2 %collective-permute-done.15 = f32[48,3,2304]{2,0,1:T(8,128)} collective-permute-done((f32[48,3,2304]{2,0,1:T(8,128)}, f32[48,3,2304]{2,0,1:T(8,128)}, u32[]{:S(2)}, u32[]{:S(2)}) %collective-permute-start.15) | collective-permute-done | bytes 1327136 | tf_op jit(solution)/shard_map/ppermute | solution.py:25
  447.1 7.3 fusion
  454.4 2.0 fusion.35
  457.6 61.1 %all-gather.2.cloned.1.call-done = f32[192,6912]{1,0:T(8,128)} async-done(((f32[48,6912]{1,0:T(8,128)}), f32[192,6912]{1,0:T(8,128)}) %all-gather.2.cloned.1.call-update) | async-done | bytes 5308432 | tf_op jit(solution)/shard_map/all_gather | solution.py:126
  518.8 7.4 %convolution_dynamic-update-slice_fusion = f32[192,192]{1,0:T(8,128)S(1)} fusion(f32[192,192]{1,0:T(8,128)S(1)} %broadcast_in_dim.213, s32[]{:T(128)S(6)} %select_n.312, f32[48,6912]{1,0:T(8,128)S(1)} %bitcast.105, f32[192,6912]{1,0:T(8,128)} %all-gather.2.cloned.1.call-done), kind=kOutput, calls=%fused_computation.50 | convolution fusion | flops 764411904 | bytes 6684676 | tf_op jit(solution)/shard_map/dot_general | solution.py:105
  526.9 143.2 %all-reduce.5.cloned.1.call-done = f32[192,192]{1,0:T(8,128)} async-done(((f32[192,192]{1,0:T(8,128)}), f32[192,192]{1,0:T(8,128)}) %all-reduce.5.cloned.1.call-update) | async-done | bytes 147472 | tf_op jit(solution)/shard_map/psum | solution.py:132
  672.2 11.7 %cholesky.50 = f32[128,128]{1,0:T(8,128)S(1)} custom-call(f32[128,128]{1,0:T(8,128)S(1)} %cholesky.121), custom_call_target="Cholesky" | custom-call | tf_op jit(solution)/shard_map/jit(cholesky)/cholesky | solution.py:133
  683.9 9.8 %custom-call.15 = f32[1,128,128]{1,2,0:T(8,128)S(1)} custom-call(f32[1,128,128]{2,1,0:T(8,128)S(1)} %get-tuple-element.28), custom_call_target="InvertDiagBlocksLowerTriangular" | custom-call | tf_op jit(solution)/shard_map/jit(cholesky)/cholesky | solution.py:133
  694.1 5.8 cholesky.108
  702.7 19.7 %custom-call.16 = f32[2,128,128]{1,2,0:T(8,128)S(1)} custom-call(f32[2,128,128]{2,1,0:T(8,128)S(1)} %pad_maximum_fusion), custom_call_target="InvertDiagBlocksLowerTriangular" | custom-call | tf_op jit(solution)/shard_map/jit(_solve_triangular)/triangular_solve | solution.py:134
  723.3 5.6 fusion.53
  (76 shorter events, 19.6 us)
Async XLA Ops:
  6.5 512.2 %all-gather.2.cloned.1.call-start = ((), (), s32[]{:S(2)}) async-start(), calls=%async_computation | async-start | bytes 6635520 | tf_op jit(solution)/shard_map/all_gather | solution.py:126
  6.5 38.5 %collective-permute-start = (f32[48,3,2304]{2,0,1:T(8,128)}, f32[48,3,2304]{2,0,1:T(8,128)}, u32[]{:S(2)}, u32[]{:S(2)}) collective-permute-start(f32[48,3,2304]{2,0,1:T(8,128)} %param.2), channel_id=1, source_target_pairs={{0,2},{1,3},{2,4},{3,5},{4,6},{5,7},{6,8},{7,9},{8,10},{9,11},{10,... | collective-permute-start | bytes 3981320 | tf_op jit(solution)/shard_map/ppermute | solution.py:25
  10.1 64.8 %collective-permute-start.1 = (f32[48,3,2304]{2,0,1:T(8,128)}, f32[48,3,2304]{2,0,1:T(8,128)}, u32[]{:S(2)}, u32[]{:S(2)}) collective-permute-start(f32[48,3,2304]{2,0,1:T(8,128)} %param.2), channel_id=1, source_target_pairs={{0,1},{1,2},{2,3},{3,4},{4,5},{5,6},{6,7},{7,8},{8,9},{9,10},{10,1... | collective-permute-start | bytes 3981320 | tf_op jit(solution)/shard_map/ppermute | solution.py:25
  10.4 68.0 %collective-permute-start.2 = (f32[48,3,2304]{2,0,1:T(8,128)}, f32[48,3,2304]{2,0,1:T(8,128)}, u32[]{:S(2)}, u32[]{:S(2)}) collective-permute-start(f32[48,3,2304]{2,0,1:T(8,128)} %param.2), channel_id=1, source_target_pairs={{0,31},{1,0},{2,1},{3,2},{4,3},{5,4},{6,5},{7,6},{8,7},{9,8},{10,9... | collective-permute-start | bytes 3981320 | tf_op jit(solution)/shard_map/ppermute | solution.py:25
  17.3 82.1 %collective-permute-start.3 = (f32[48,3,2304]{2,0,1:T(8,128)}, f32[48,3,2304]{2,0,1:T(8,128)}, u32[]{:S(2)}, u32[]{:S(2)}) collective-permute-start(f32[48,3,2304]{2,0,1:T(8,128)} %param.2), channel_id=1, source_target_pairs={{0,30},{1,31},{2,0},{3,1},{4,2},{5,3},{6,4},{7,5},{8,6},{9,7},{10,... | collective-permute-start | bytes 3981320 | tf_op jit(solution)/shard_map/ppermute | solution.py:25
  81.8 21.1 %copy-start.8 = (f32[48,3,2304]{2,1,0:T(4,128)S(1)}, f32[48,3,2304]{2,1,0:T(4,128)}, u32[]{:S(2)}) copy-start(f32[48,3,2304]{2,1,0:T(4,128)} %copy.118) | copy-start | bytes 3981316
  153.6 5.7 copy-start.3
  153.6 5.7 copy-start.10
  161.5 35.4 %collective-permute-start.4 = (f32[48,3,2304]{2,0,1:T(8,128)}, f32[48,3,2304]{2,0,1:T(8,128)}, u32[]{:S(2)}, u32[]{:S(2)}) collective-permute-start(f32[48,3,2304]{2,0,1:T(8,128)} %get-tuple-element.25), channel_id=1, source_target_pairs={{0,2},{1,3},{2,4},{3,5},{4,6},{5,7},{6,8},{7,9},{8,10},{9,11},{10,... | collective-permute-start | bytes 3981320 | tf_op jit(solution)/shard_map/ppermute | solution.py:25
  164.3 65.0 %collective-permute-start.5 = (f32[48,3,2304]{2,0,1:T(8,128)}, f32[48,3,2304]{2,0,1:T(8,128)}, u32[]{:S(2)}, u32[]{:S(2)}) collective-permute-start(f32[48,3,2304]{2,0,1:T(8,128)} %get-tuple-element.25), channel_id=1, source_target_pairs={{0,1},{1,2},{2,3},{3,4},{4,5},{5,6},{6,7},{7,8},{8,9},{9,10},{10,1... | collective-permute-start | bytes 3981320 | tf_op jit(solution)/shard_map/ppermute | solution.py:25
  165.2 65.6 %collective-permute-start.6 = (f32[48,3,2304]{2,0,1:T(8,128)}, f32[48,3,2304]{2,0,1:T(8,128)}, u32[]{:S(2)}, u32[]{:S(2)}) collective-permute-start(f32[48,3,2304]{2,0,1:T(8,128)} %get-tuple-element.25), channel_id=1, source_target_pairs={{0,31},{1,0},{2,1},{3,2},{4,3},{5,4},{6,5},{7,6},{8,7},{9,8},{10,9... | collective-permute-start | bytes 3981320 | tf_op jit(solution)/shard_map/ppermute | solution.py:25
  172.1 77.3 %collective-permute-start.7 = (f32[48,3,2304]{2,0,1:T(8,128)}, f32[48,3,2304]{2,0,1:T(8,128)}, u32[]{:S(2)}, u32[]{:S(2)}) collective-permute-start(f32[48,3,2304]{2,0,1:T(8,128)} %get-tuple-element.25), channel_id=1, source_target_pairs={{0,30},{1,31},{2,0},{3,1},{4,2},{5,3},{6,4},{7,5},{8,6},{9,7},{10,... | collective-permute-start | bytes 3981320 | tf_op jit(solution)/shard_map/ppermute | solution.py:25
  198.4 32.3 %copy-start.2 = (f32[48,3,2304]{2,0,1:T(8,128)S(1)}, f32[48,3,2304]{2,0,1:T(8,128)}, u32[]{:S(2)}) copy-start(f32[48,3,2304]{2,0,1:T(8,128)} %get-tuple-element.26) | copy-start | bytes 3981316
  250.8 7.4 %copy-start.4 = (f32[48,3,2304]{2,0,1:T(8,128)S(1)}, f32[48,3,2304]{2,0,1:T(8,128)}, u32[]{:S(2)}) copy-start(f32[48,3,2304]{2,0,1:T(8,128)} %param.2) | copy-start | bytes 3981316
  250.8 7.4 %copy-start.6 = (f32[48,3,2304]{2,1,0:T(4,128)S(1)}, f32[48,3,2304]{2,1,0:T(4,128)}, u32[]{:S(2)}) copy-start(f32[48,3,2304]{2,1,0:T(4,128)} %reshape.101) | copy-start | bytes 3981316
  250.9 7.4 %copy-start.12 = (f32[3,2304]{1,0:T(4,128)S(1)}, f32[3,2304]{1,0:T(4,128)}, u32[]{:S(2)}) copy-start(f32[3,2304]{1,0:T(4,128)} %broadcast_multiply_fusion.2) | copy-start | bytes 82948
  258.9 34.4 %collective-permute-start.8 = (f32[48,3,2304]{2,0,1:T(8,128)S(1)}, f32[48,3,2304]{2,0,1:T(8,128)}, u32[]{:S(2)}, u32[]{:S(2)}) collective-permute-start(f32[48,3,2304]{2,0,1:T(8,128)S(1)} %fusion.45), channel_id=1, source_target_pairs={{0,2},{1,3},{2,4},{3,5},{4,6},{5,7},{6,8},{7,9},{8,10},{9,11},{10,... | collective-permute-start | bytes 3981320 | tf_op jit(solution)/shard_map/ppermute | solution.py:25
  261.7 65.7 %collective-permute-start.9 = (f32[48,3,2304]{2,0,1:T(8,128)S(1)}, f32[48,3,2304]{2,0,1:T(8,128)}, u32[]{:S(2)}, u32[]{:S(2)}) collective-permute-start(f32[48,3,2304]{2,0,1:T(8,128)S(1)} %fusion.45), channel_id=1, source_target_pairs={{0,1},{1,2},{2,3},{3,4},{4,5},{5,6},{6,7},{7,8},{8,9},{9,10},{10,1... | collective-permute-start | bytes 3981320 | tf_op jit(solution)/shard_map/ppermute | solution.py:25
  262.1 66.9 %collective-permute-start.10 = (f32[48,3,2304]{2,0,1:T(8,128)S(1)}, f32[48,3,2304]{2,0,1:T(8,128)}, u32[]{:S(2)}, u32[]{:S(2)}) collective-permute-start(f32[48,3,2304]{2,0,1:T(8,128)S(1)} %fusion.45), channel_id=1, source_target_pairs={{0,31},{1,0},{2,1},{3,2},{4,3},{5,4},{6,5},{7,6},{8,7},{9,8},{10,9... | collective-permute-start | bytes 3981320 | tf_op jit(solution)/shard_map/ppermute | solution.py:25
  268.9 80.1 %collective-permute-start.11 = (f32[48,3,2304]{2,0,1:T(8,128)S(1)}, f32[48,3,2304]{2,0,1:T(8,128)}, u32[]{:S(2)}, u32[]{:S(2)}) collective-permute-start(f32[48,3,2304]{2,0,1:T(8,128)S(1)} %fusion.45), channel_id=1, source_target_pairs={{0,30},{1,31},{2,0},{3,1},{4,2},{5,3},{6,4},{7,5},{8,6},{9,7},{10,... | collective-permute-start | bytes 3981320 | tf_op jit(solution)/shard_map/ppermute | solution.py:25
  272.6 5.3 copy-start
  350.4 7.4 copy-start.7
  350.4 7.4 copy-start.11
  359.6 33.6 %collective-permute-start.12 = (f32[48,3,2304]{2,0,1:T(8,128)}, f32[48,3,2304]{2,0,1:T(8,128)}, u32[]{:S(2)}, u32[]{:S(2)}) collective-permute-start(f32[48,3,2304]{2,0,1:T(8,128)} %fusion.40), channel_id=1, source_target_pairs={{0,2},{1,3},{2,4},{3,5},{4,6},{5,7},{6,8},{7,9},{8,10},{9,11},{10,... | collective-permute-start | bytes 3981320 | tf_op jit(solution)/shard_map/ppermute | solution.py:25
  362.6 66.6 %collective-permute-start.13 = (f32[48,3,2304]{2,0,1:T(8,128)}, f32[48,3,2304]{2,0,1:T(8,128)}, u32[]{:S(2)}, u32[]{:S(2)}) collective-permute-start(f32[48,3,2304]{2,0,1:T(8,128)} %fusion.40), channel_id=1, source_target_pairs={{0,1},{1,2},{2,3},{3,4},{4,5},{5,6},{6,7},{7,8},{8,9},{9,10},{10,1... | collective-permute-start | bytes 3981320 | tf_op jit(solution)/shard_map/ppermute | solution.py:25
  362.6 69.4 %collective-permute-start.14 = (f32[48,3,2304]{2,0,1:T(8,128)}, f32[48,3,2304]{2,0,1:T(8,128)}, u32[]{:S(2)}, u32[]{:S(2)}) collective-permute-start(f32[48,3,2304]{2,0,1:T(8,128)} %fusion.40), channel_id=1, source_target_pairs={{0,31},{1,0},{2,1},{3,2},{4,3},{5,4},{6,5},{7,6},{8,7},{9,8},{10,9... | collective-permute-start | bytes 3981320 | tf_op jit(solution)/shard_map/ppermute | solution.py:25
  369.8 75.9 %collective-permute-start.15 = (f32[48,3,2304]{2,0,1:T(8,128)}, f32[48,3,2304]{2,0,1:T(8,128)}, u32[]{:S(2)}, u32[]{:S(2)}) collective-permute-start(f32[48,3,2304]{2,0,1:T(8,128)} %fusion.40), channel_id=1, source_target_pairs={{0,30},{1,31},{2,0},{3,1},{4,2},{5,3},{6,4},{7,5},{8,6},{9,7},{10,... | collective-permute-start | bytes 3981320 | tf_op jit(solution)/shard_map/ppermute | solution.py:25
  374.3 5.3 copy-start.1
  457.5 61.2 %copy-start.5 = (f32[3,6,8,2304]{3,2,0,1:T(8,128)S(1)}, f32[3,6,8,2304]{3,2,0,1:T(8,128)}, u32[]{:S(2)}) copy-start(f32[3,6,8,2304]{3,2,0,1:T(8,128)} %copy.168) | copy-start | bytes 3981316
  457.5 212.6 %all-reduce.5.cloned.1.call-start = ((), (), s32[]{:S(2)}) async-start(), calls=%async_computation.1 | async-start | bytes 393216 | tf_op jit(solution)/shard_map/psum | solution.py:132
  526.2 0.7 copy-start.9
Sparse Core Ops, SparseCore 0:
  457.7 61.0 all-gather.1
  527.0 143.0 all-reduce.4
where the time goes:
time: 748 us; the launch traced here: 737 us
  waiting for transfers between devices  419 us (56%)
  local copies, waits for them, and re-layouts  124 us (17%)
  matrix products  79 us (11%)
  other arithmetic  57.7 us (8%)
  starting transfers between devices  41.7 us (6%)
  between operations  15.7 us (2%)
    ppermute x16, waiting for transfers between devices, from_behind(): lax.ppermute(value, axis, [(i, (i + by) % peers) for i in range(peers)])  215 us
    psum x1, waiting for transfers between devices, per_device(): intersection = lax.psum(partial_value, ('band', 'dom')) / cell_count  143 us
    all_gather x1, waiting for transfers between devices, per_device(): everyone = lax.all_gather(flattened, 'band', axis=0, tiled=True)  61.1 us
    concatenate x4, local copies, waits for them, and re-layouts, assemble(): return jnp.concatenate([lower, field, upper], axis=1)  55 us
    ppermute x16, starting transfers between devices, from_behind(): lax.ppermute(value, axis, [(i, (i + by) % peers) for i in range(peers)])  41.6 us
    another operation x7, other arithmetic, per_device(): lower_factor = jnp.linalg.cholesky(intersection)  28.7 us
    dot_general x4, matrix products, apply_hamiltonian(): jnp.einsum('rpc,pq->rqc', padded, across_x, precision=lax.Precision.HIGHE...  27.7 us
    dot_general x4, matrix products, apply_hamiltonian(): jnp.einsum('rxyz,yw->rxwz', grid, across_y, precision=lax.Precision.HIGHE...  20 us
  transfers between devices with their start and end apart: 18, of which 14 were waited for; matrix products, arithmetic and copies ran while one was open for 14% of the time, Pallas kernels for 0%

commit v1 on v0

v1 whole, which is shorter than its diff:
```python
import functools

import jax
import jax.numpy as jnp
import numpy as np
from jax import lax
from jax.experimental import pallas as pl
from jax.experimental.pallas import tpu as pltpu
from jax.sharding import PartitionSpec as P

M = 192
CELLS = 221184
MESH = pl.DeviceIdType.MESH

stencil_weights = (
    -5369.0 / 1800.0,
    12.0 / 7.0,
    -15.0 / 56.0,
    10.0 / 189.0,
    -1.0 / 112.0,
    2.0 / 1925.0,
    -1.0 / 16632.0,
)
SCALE = 0.4
COEFS = [-0.5 * SCALE * w for w in stencil_weights]
DIAGONAL = 3.0 * COEFS[0] - 7.0 * SCALE
TILES = 14


def z_matrix():
    full = np.zeros((128, 128), np.float32)
    for slot in range(2):
        for z in range(48):
            for k in range(1, 7):
                full[slot * 64 + z, slot * 64 + (z + k) % 48] += COEFS[k]
                full[slot * 64 + z, slot * 64 + (z - k) % 48] += COEFS[k]
    high = full.astype(jnp.bfloat16)
    low = (full - high.astype(np.float32)).astype(jnp.bfloat16)
    row = np.concatenate([high, low], 1)
    return np.concatenate([row, row], 0)


def roll_lanes(v, by):
    by = by % 128
    return v if by == 0 else pltpu.roll(v, by, 1)


def lane_index():
    return lax.broadcasted_iota(jnp.int32, (8, 128), 1)


def unpack_y(tiles, y, shift):
    start = 48 * y
    tile, off = start // 128, start % 128
    first = roll_lanes(tiles[tile], shift - off)
    if off + 48 <= 128:
        return first
    taken = 128 - off
    second = roll_lanes(tiles[tile + 1], shift + taken)
    return jnp.where(lane_index() < shift + taken, first, second)


def pack_tile(rows, tile, shift):
    out = None
    for y in range(8):
        start = 48 * y
        lo, hi = max(start, tile * 128), min(start + 48, tile * 128 + 128)
        if lo >= hi:
            continue
        piece = roll_lanes(rows[y], start - tile * 128 - shift)
        out = piece if out is None else jnp.where(lane_index() < lo - tile * 128, out, piece)
    return out


def kernel(x_ref, p_ref, w_ref, g_ref, e_ref, recv, pot_in, field_a, field_b, pot, pack,
           part, rs_buf, xy_buf, sums, gsum, send_sems, recv_sems):
    b = lax.axis_index("band")
    d = lax.axis_index("dom")
    core = lax.rem(b, 2)
    y_pos, zh, x_pos = d // 8, lax.rem(d // 4, 2), lax.rem(d, 4)
    odd = lax.rem(d, 2)
    pair = d // 2
    two = lax.rem(core + d, 2) == 0
    first = 3 * pair + odd * (2 - core)
    me = d * 4 + b

    barrier = pltpu.get_barrier_semaphore()

    def greet(i, c):
        to = lax.rem(me + i, 128)
        pl.semaphore_signal(barrier, inc=1, device_id=(lax.rem(to, 4), to // 4), device_id_type=MESH)
        return c

    lax.fori_loop(1, 128, greet, 0)
    pl.semaphore_wait(barrier, 127)

    def piece(o):
        p = o // 3
        r = lax.rem(o, 3)
        to = 2 * p + jnp.where(r >= 2 - core, 1, 0)
        slot = jnp.where(core == 0, jnp.where(r == 1, 1, 0), jnp.where(r == 2, 1, 0))
        return to, slot

    def send_orbital(i, c):
        o = lax.rem(first + 2 + i, 48)
        to, slot = piece(o)
        src = x_ref.at[:, o, :]
        dst = recv.at[slot, lax.rem(d, 4), :, d // 4, :]

        @pl.when(to == d)
        def _():
            pltpu.make_async_copy(src, dst, recv_sems.at[slot]).start()

        @pl.when(to != d)
        def _():
            pltpu.make_async_remote_copy(
                src_ref=src, dst_ref=dst, send_sem=send_sems.at[0], recv_sem=recv_sems.at[slot],
                device_id=(b, to), device_id_type=MESH).start()
        return c

    lax.fori_loop(0, 48, send_orbital, 0)
    pot_dst = pot_in.at[lax.rem(d, 4), :, d // 4, :]
    pltpu.make_async_copy(p_ref, pot_dst, recv_sems.at[2]).start()

    def send_potential(i, c):
        to = lax.rem(d + i, 32)
        pltpu.make_async_remote_copy(
            src_ref=p_ref, dst_ref=pot_dst, send_sem=send_sems.at[1], recv_sem=recv_sems.at[2],
            device_id=(b, to), device_id_type=MESH).start()
        return c

    lax.fori_loop(1, 32, send_potential, 0)

    pltpu.make_async_copy(recv.at[0], recv.at[0], recv_sems.at[0]).wait()

    @pl.when(two)
    def _():
        pltpu.make_async_copy(recv.at[1], recv.at[1], recv_sems.at[1]).wait()

    @pl.when(jnp.logical_not(two))
    def _():
        recv[1] = jnp.zeros_like(recv[1])

    pltpu.make_async_copy(pot_in, pot_in, recv_sems.at[2]).wait()

    def unpack(n, c):
        yb = n // 12
        xi = lax.rem(n, 12)
        q, j = xi // 3, lax.rem(xi, 3)
        lanes = [pl.ds(pl.multiple_of(yb * 384 + 128 * t, 128), 128) for t in range(3)]
        left = [recv[0, q, j, :, s] for s in lanes]
        right = [recv[1, q, j, :, s] for s in lanes]
        potential = [pot_in[q, j, :, s] for s in lanes]
        lane = lane_index()
        rows = pl.ds(pl.multiple_of(xi * 8, 8), 8)
        for y in range(8):
            both = jnp.where(lane < 64, unpack_y(left, y, 0), unpack_y(right, y, 64))
            field_a[yb * 8 + y, rows, :] = both
            v = jnp.where(lane < 64, unpack_y(potential, y, 0), unpack_y(potential, y, 64))
            pot[yb * 8 + y, rows, :] = v * SCALE + DIAGONAL
        return c

    lax.fori_loop(0, 72, unpack, 0)

    def step(src, dst, is_first):
        def row(y, c):
            own = src[y]
            high = own.astype(jnp.bfloat16)
            low = (own - high.astype(jnp.float32)).astype(jnp.bfloat16)
            along_z = jnp.dot(jnp.concatenate([high, low], 1), w_ref[...],
                              preferred_element_type=jnp.float32)
            regs = [own[8 * i:8 * i + 8] for i in range(12)]
            before = {i: pltpu.roll(regs[i], 1, 0) for i in range(6, 12)}
            after = {i: pltpu.roll(regs[i], 7, 0) for i in range(6)}
            at = lambda i: before[i + 12] if i < 0 else (after[i - 12] if i >= 12 else regs[i])
            up = [lax.rem(y + k, 48) for k in range(1, 7)]
            down = [lax.rem(y + 48 - k, 48) for k in range(1, 7)]
            for i in range(12):
                rows = pl.ds(8 * i, 8)
                acc = regs[i] * pot[y, rows, :]
                acc = acc + (along_z[8 * i:8 * i + 8, :128] + along_z[8 * i:8 * i + 8, 128:])
                for k in range(1, 7):
                    near = (at(i + k) + at(i - k)) + (src[up[k - 1], rows, :] + src[down[k - 1], rows, :])
                    acc = acc + COEFS[k] * near
                dst[y, rows, :] = 0.5 * acc if is_first else acc - dst[y, rows, :]
            return c

        lax.fori_loop(0, 48, row, 0)

    step(field_a, field_b, True)
    step(field_b, field_a, False)
    step(field_a, field_b, False)
    step(field_b, field_a, False)

    def repack(n, c):
        yb = n // 12
        xi = lax.rem(n, 12)
        q, j = xi // 3, lax.rem(xi, 3)
        rows = [field_a[yb * 8 + y, pl.ds(pl.multiple_of(xi * 8, 8), 8), :] for y in range(8)]
        for t in range(3):
            for slot in range(2):
                pack[q, j * 18 + yb * 3 + t, slot] = pack_tile(rows, t, 64 * slot)
        return c

    lax.fori_loop(0, 72, repack, 0)

    def spread(count):
        def send(i, c):
            to = lax.rem(me + i, 128)
            to_b, to_d = lax.rem(to, 4), to // 4
            begin = 14 * to_b - jnp.maximum(to_b - 1, 0)
            src = pack.at[lax.rem(to_d, 4), pl.ds(begin, TILES), pl.ds(0, count), to_d // 4, :]
            dst = e_ref.at[to_b, :, pl.ds(48 * b + first, count), :]
            pltpu.make_async_remote_copy(
                src_ref=src, dst_ref=dst, send_sem=send_sems.at[2], recv_sem=recv_sems.at[3],
                device_id=(to_b, to_d), device_id_type=MESH).start()
            return c

        lax.fori_loop(1, 128, send, 0)
        begin = 14 * b - jnp.maximum(b - 1, 0)
        pltpu.make_async_copy(
            pack.at[lax.rem(d, 4), pl.ds(begin, TILES), pl.ds(0, count), d // 4, :],
            e_ref.at[b, :, pl.ds(48 * b + first, count), :], recv_sems.at[3]).start()

    @pl.when(two)
    def _():
        spread(2)

    @pl.when(jnp.logical_not(two))
    def _():
        spread(1)

    pltpu.make_async_copy(e_ref.at[b], e_ref.at[b], recv_sems.at[3]).wait()

    for i in range(1, 4):
        to = lax.rem(b + i, 4)
        pltpu.make_async_remote_copy(
            src_ref=e_ref.at[b], dst_ref=e_ref.at[b], send_sem=send_sems.at[3],
            recv_sem=recv_sems.at[7 + i], device_id=(to, d), device_id_type=MESH).start()

    def gram(left, right):
        return lax.dot_general(left, right, (((1,), (1,)), ((), ())), precision=lax.Precision.HIGHEST,
                               preferred_element_type=jnp.float32)

    total = jnp.zeros((M, M), jnp.float32)
    for i in range(0, TILES, 2):
        one = e_ref[b, i]
        if i == 0:
            one = jnp.where(b >= 2, 0.0, one)
        both = jnp.concatenate([one, e_ref[b, i + 1]], 1)
        total = total + gram(both, both)
    part[:, :, 0:128] = total[:, :128].reshape(8, 24, 128)
    part[:, :, 128:256] = jnp.concatenate([total[:, 128:], jnp.zeros((M, 64), jnp.float32)], 1).reshape(8, 24, 128)

    mine = zh * 4 + b
    rs_buf[mine] = part[mine]
    for i in range(1, 8):
        to = lax.rem(mine + i, 8)
        pltpu.make_async_remote_copy(
            src_ref=part.at[to], dst_ref=rs_buf.at[mine], send_sem=send_sems.at[4], recv_sem=recv_sems.at[4],
            device_id=(lax.rem(to, 4), y_pos * 8 + (to // 4) * 4 + x_pos), device_id_type=MESH).start()
    pltpu.make_async_copy(rs_buf.at[pl.ds(0, 7)], rs_buf.at[pl.ds(0, 7)], recv_sems.at[4]).wait()
    acc = rs_buf[0]
    for i in range(1, 8):
        acc = acc + rs_buf[i]
    sums[...] = acc
    spot = y_pos * 4 + x_pos
    xy_buf[spot] = acc
    for i in range(1, 16):
        to = lax.rem(spot + i, 16)
        pltpu.make_async_remote_copy(
            src_ref=sums, dst_ref=xy_buf.at[spot], send_sem=send_sems.at[5], recv_sem=recv_sems.at[5],
            device_id=(b, (to // 4) * 8 + zh * 4 + lax.rem(to, 4)), device_id_type=MESH).start()
    pltpu.make_async_copy(xy_buf.at[pl.ds(0, 15)], xy_buf.at[pl.ds(0, 15)], recv_sems.at[5]).wait()
    acc = xy_buf[0]
    for i in range(1, 16):
        acc = acc + xy_buf[i]
    gsum[...] = acc
    g_ref[mine] = acc
    for i in range(1, 8):
        to = lax.rem(mine + i, 8)
        pltpu.make_async_remote_copy(
            src_ref=gsum, dst_ref=g_ref.at[mine], send_sem=send_sems.at[6], recv_sem=recv_sems.at[6],
            device_id=(lax.rem(to, 4), y_pos * 8 + (to // 4) * 4 + x_pos), device_id_type=MESH).start()
    pltpu.make_async_copy(g_ref.at[pl.ds(0, 7)], g_ref.at[pl.ds(0, 7)], recv_sems.at[6]).wait()

    for i in range(1, 4):
        pltpu.make_async_copy(e_ref.at[b], e_ref.at[b], recv_sems.at[7 + i]).wait()

    def drain(ref, sem, times):
        def body(i, c):
            pltpu.make_async_copy(ref, ref, sem).wait()
            return c
        lax.fori_loop(0, times, body, 0)

    orbital = recv.at[0, 0, :, 0, :]
    drain(orbital, send_sems.at[0], jnp.where(two, 46, 47))
    drain(orbital, send_sems.at[1], 31)
    share = pack.at[0, pl.ds(0, TILES), pl.ds(0, 1), 0, :]
    drain(share, send_sems.at[2], jnp.where(two, 254, 127))
    drain(e_ref.at[0], send_sems.at[3], 3)
    drain(part.at[0], send_sems.at[4], 7)
    drain(sums, send_sems.at[5], 15)
    drain(sums, send_sems.at[6], 7)


def per_device(orbitals, potential):
    f32 = jnp.float32
    vmem = pl.BlockSpec(memory_space=pltpu.VMEM)
    g, e = pl.pallas_call(
        kernel,
        out_shape=(jax.ShapeDtypeStruct((8, 24, 256), f32),
                   jax.ShapeDtypeStruct((4, TILES, M, 128), f32)),
        in_specs=[pl.BlockSpec(memory_space=pl.ANY), vmem, vmem],
        out_specs=(vmem, vmem),
        scratch_shapes=[
            pltpu.VMEM((2, 4, 3, 8, 2304), f32),
            pltpu.VMEM((4, 3, 8, 2304), f32),
            pltpu.VMEM((48, 96, 128), f32),
            pltpu.VMEM((48, 96, 128), f32),
            pltpu.VMEM((48, 96, 128), f32),
            pltpu.VMEM((4, 54, 2, 8, 128), f32),
            pltpu.VMEM((8, 24, 256), f32),
            pltpu.VMEM((8, 24, 256), f32),
            pltpu.VMEM((16, 24, 256), f32),
            pltpu.VMEM((24, 256), f32),
            pltpu.VMEM((24, 256), f32),
            pltpu.SemaphoreType.DMA((7,)),
            pltpu.SemaphoreType.DMA((11,)),
        ],
        compiler_params=pltpu.CompilerParams(
            collective_id=0, has_side_effects=True, vmem_limit_bytes=48 * 2**20),
    )(jnp.transpose(orbitals, (1, 0, 2)), potential, jnp.asarray(z_matrix()))
    intersection = g.reshape(M, 256)[:, :M] / CELLS
    lower = jnp.linalg.cholesky(intersection)
    inverse = jax.scipy.linalg.solve_triangular(lower, jnp.eye(M, dtype=f32), lower=True)
    own = lax.dynamic_slice_in_dim(inverse, lax.axis_index("band") * 48, 48, 0)
    everyone = jnp.concatenate([e[0], e[1], e[2, 1:], e[3, 1:]], 0)
    out = jnp.einsum("ij,tjc->tic", own, everyone, precision=lax.Precision.HIGHEST,
                     preferred_element_type=f32)
    return out.reshape(3, 18, 48, 128).transpose(2, 0, 1, 3).reshape(48, 3, 2304)


def solution(mesh):
    placed = (P("band", "dom", None), P("dom", None))
    return jax.shard_map(
        per_device, mesh=mesh, in_specs=placed, out_specs=P("band", "dom", None), check_vma=False
    )
```

time: 748 us -> 257 us (0.34); the launches traced: 737 us -> 256 us
  waiting for transfers between devices: 419 us -> 0 us
  Pallas kernels: 0 us -> 189 us
  local copies, waits for them, and re-layouts: 124 us -> 10.5 us
  matrix products: 79 us -> 6.39 us
  starting transfers between devices: 41.7 us -> 0 us
  between operations: 15.7 us -> 1.45 us
  other arithmetic: 57.7 us -> 49.3 us
    ppermute x16 -> x0, waiting for transfers between devices: 215 us -> none  [from_behind(): lax.ppermute(value, axis, [(i, (i + by) % peers) for i in range(peers)])]
    pallas_call x0 -> x1, Pallas kernels: none -> 189 us  [per_device(): pl.pallas_call(kernel, out_shape=(jax.ShapeDtypeStruct((8, 24, 256), f32)...]
    psum x1 -> x0, waiting for transfers between devices: 143 us -> none  [per_device(): intersection = lax.psum(partial_value, ('band', 'dom')) / cell_count]
    dot_general x14 -> x1, matrix products: 77.7 us -> 5.08 us  [per_device(): jnp.einsum('ij,tjc->tic', own, everyone, precision=lax.Precision.HIGHEST,...]
    all_gather x1 -> x0, waiting for transfers between devices: 61.1 us -> none  [per_device(): everyone = lax.all_gather(flattened, 'band', axis=0, tiled=True)]
    concatenate x4 -> x0, local copies, waits for them, and re-layouts: 55 us -> none  [assemble(): return jnp.concatenate([lower, field, upper], axis=1)]
    ppermute x16 -> x0, starting transfers between devices: 41.6 us -> none  [from_behind(): lax.ppermute(value, axis, [(i, (i + by) % peers) for i in range(peers)])]
    reshape x10 -> x2, local copies, waits for them, and re-layouts: 36.8 us -> 1.73 us  [per_device(): out.reshape(3, 18, 48, 128).transpose(2, 0, 1, 3).reshape(48, 3, 2304)]
  transfers between devices with their start and end apart: 18 -> 0, of which waited for: 14 -> 0; matrix products, arithmetic and copies ran while one was open for 14% -> 0% of each run, Pallas kernels for 0% -> 0%
where the time goes in v1:
time: 257 us; the launch traced here: 256 us
  Pallas kernels  189 us (74%)
  other arithmetic  49.3 us (19%)
  local copies, waits for them, and re-layouts  10.5 us (4%)
  matrix products  6.39 us (2%)
    pallas_call x1, Pallas kernels, per_device(): pl.pallas_call(kernel, out_shape=(jax.ShapeDtypeStruct((8, 24, 256), f32)...  189 us
    another operation x7, other arithmetic, per_device(): lower = jnp.linalg.cholesky(intersection)  28.8 us
    another operation x6, other arithmetic, per_device(): jax.scipy.linalg.solve_triangular(lower, jnp.eye(M, dtype=f32), lower=True)  19.8 us
    squeeze x2, local copies, waits for them, and re-layouts, per_device(): everyone = jnp.concatenate([e[0], e[1], e[2, 1:], e[3, 1:]], 0)  5.51 us

profile of v1, /device:TPU:1, one launch (start us, length us, event | category | flops | bytes accessed | tf_op | source)
XLA Modules:
  0.0 256.3 jit_solution(932689915627680727)
XLA Ops:
  0.0 0.0 copy-start
  0.0 1.3 copy-done
  1.3 0.0 copy-start.1
  1.3 0.9 copy-done.1
  2.2 0.0 copy-start.2
  2.2 0.8 copy-done.2
  3.0 188.7 %shard_map.37 = (f32[8,24,256]{2,1,0:T(8,128)S(1)}, f32[4,14,192,128]{3,2,1,0:T(8,128)}) custom-call(f32[3,48,2304]{2,1,0:T(8,128)S(1)} %bitcast.47, f32[3,2304]{1,0:T(4,128)S(1)} %copy-done.2, bf16[256,256]{1,0:T(8,128)(2,1)S(1)} %copy-done.1), custom_call_target="tpu_custom_call" | custom-call | tf_op jit(solution)/shard_map/pallas_call | solution.py:310
  191.7 3.5 %slice_bitcast_fusion.3 = (f32[13,192,128]{2,1,0:T(8,128)}, f32[13,192,128]{2,1,0:T(8,128)}) fusion(f32[4,14,192,128]{3,2,1,0:T(8,128)} %get-tuple-element.7), kind=kLoop, calls=%fused_computation.12 | loop fusion | bytes 5111808 | tf_op jit(solution)/shard_map/squeeze | solution.py:338
  195.2 2.0 slice_bitcast_fusion.1
  197.2 0.6 iota_compare_fusion
  197.9 0.1 copy.14
  198.0 0.1 copy.9
  198.2 0.0 copy-start.3
  198.2 11.7 %cholesky.51 = f32[128,128]{1,0:T(8,128)S(1)} custom-call(f32[128,128]{1,0:T(8,128)S(1)} %cholesky.124), custom_call_target="Cholesky" | custom-call | tf_op jit(solution)/shard_map/jit(cholesky)/cholesky | solution.py:335
  210.0 9.8 %custom-call.15 = f32[1,128,128]{1,2,0:T(8,128)S(1)} custom-call(f32[1,128,128]{2,1,0:T(8,128)S(1)} %get-tuple-element.34), custom_call_target="InvertDiagBlocksLowerTriangular" | custom-call | tf_op jit(solution)/shard_map/jit(cholesky)/cholesky | solution.py:335
  219.8 0.2 constant_dynamic-update-slice_fusion
  220.0 0.2 convolution_subtract_fusion.1
  220.2 5.8 %cholesky.110 = f32[64,64]{1,0:T(8,128)S(1)} custom-call(f32[64,64]{1,0:T(8,128)S(1)} %convolution_subtract_fusion.1), custom_call_target="Cholesky" | custom-call | tf_op jit(solution)/shard_map/jit(cholesky)/cholesky | solution.py:335
  226.0 0.7 compare_reduce_fusion.1
  226.8 0.7 compare_reduce_fusion
  228.7 0.1 fusion.14
  228.8 19.7 %custom-call.16 = f32[2,128,128]{1,2,0:T(8,128)S(1)} custom-call(f32[2,128,128]{2,1,0:T(8,128)S(1)} %pad_maximum_fusion), custom_call_target="InvertDiagBlocksLowerTriangular" | custom-call | tf_op jit(solution)/shard_map/jit(_solve_triangular)/triangular_solve | solution.py:336
  248.5 0.0 copy-done.3
  248.5 0.3 fusion.9
  248.8 0.3 convolution_subtract_fusion
  249.1 0.3 fusion.18
  249.5 5.1 %fusion = f32[54,128,48]{1,2,0:T(8,128)S(1)} fusion(f32[13,192,128]{2,1,0:T(8,128)} %get-tuple-element.32, f32[13,192,128]{2,1,0:T(8,128)} %get-tuple-element.31, f32[14,192,128]{2,1,0:T(8,128)S(1)} %get-tuple-element.30, f32[14,192,128]{2,1,0:T(8,128)S(1)} %get-tuple-element.29, s32[]{:T(128)S(6)} %select_n.8, f32[128,192]{0,1:T(8,128)S(1)} %fusion.9, ...), kind=kOutput, calls=%fused_computation | convolution fusion | flops 768402432 | bytes 6782980 | tf_op jit(solution)/shard_map/ij,tjc->tic/dot_general | solution.py:339
  254.6 0.5 copy.16
  255.0 1.3 reshape.34
  (11 shorter events, 0.2 us)
Async XLA Ops:
  0.0 1.3 copy-start
  1.3 0.9 copy-start.1
  2.2 0.8 copy-start.2
  198.2 50.4 %copy-start.3 = (pred[192,192]{1,0:T(32,128)(4,1)S(1)}, pred[192,192]{1,0:T(32,128)(4,1)}, u32[]{:S(2)}) copy-start(pred[192,192]{1,0:T(32,128)(4,1)} %iota_compare_fusion) | copy-start | bytes 110596

commit v2 on v1

v2 whole, which is shorter than its diff:
```python
import jax
import jax.numpy as jnp
import numpy as np
from jax import lax
from jax.experimental import pallas as pl
from jax.experimental.pallas import tpu as pltpu
from jax.sharding import PartitionSpec as P

M = 192
CELLS = 221184
MESH = pl.DeviceIdType.MESH
F32, BF16 = jnp.float32, jnp.bfloat16

stencil_weights = (
    -5369.0 / 1800.0,
    12.0 / 7.0,
    -15.0 / 56.0,
    10.0 / 189.0,
    -1.0 / 112.0,
    2.0 / 1925.0,
    -1.0 / 16632.0,
)
SCALE = 0.4
COEFS = [-0.5 * SCALE * w for w in stencil_weights]
DIAGONAL = 3.0 * COEFS[0] - 7.0 * SCALE
TILES = 14
ROWS = 8


def two_terms(full):
    high = full.astype(BF16)
    return high, (full - high.astype(np.float32)).astype(BF16)


def z_matrix():
    full = np.zeros((128, 128), np.float32)
    for slot in range(2):
        for z in range(48):
            for k in range(1, 7):
                full[slot * 64 + z, slot * 64 + (z + k) % 48] += COEFS[k]
                full[slot * 64 + z, slot * 64 + (z - k) % 48] += COEFS[k]
    row = np.concatenate(two_terms(full), 1)
    return np.concatenate([row, row], 0)


def x_matrix():
    full = np.zeros((96, 96), np.float32)
    place = [(r % 8) * 12 + r // 8 for r in range(96)]
    for a in range(96):
        for c in range(96):
            away = (place[a] - place[c]) % 96
            away = min(away, 96 - away)
            if 1 <= away <= 6:
                full[a, c] = COEFS[away]
    high, low = two_terms(full)
    return np.concatenate([np.concatenate([high, high], 1), np.concatenate([low, low], 1)], 0)


def roll_lanes(v, by):
    by = by % 128
    return v if by == 0 else pltpu.roll(v, by, 1)


def lane_index():
    return lax.broadcasted_iota(jnp.int32, (8, 128), 1)


def to_rows(left, right):
    lane = lane_index()
    turned = [roll_lanes(v, 64) for v in right]
    rows = []
    for y in range(8):
        tile, off = 48 * y // 128, 48 * y % 128
        if off + 48 <= 128:
            inside = jnp.logical_and(lane >= off, lane < off + 48)
            mixed = jnp.where(inside, left[tile], turned[tile])
        else:
            mixed = jnp.where(lane < 64, turned[tile], turned[tile + 1])
            mixed = jnp.where(lane < off - 80, left[tile + 1], mixed)
            mixed = jnp.where(lane >= off, left[tile], mixed)
        rows.append(roll_lanes(mixed, -off))
    return rows


def to_tiles(rows):
    lane = lane_index()
    turned_lane = lax.rem(lane + 64, 128)
    placed = [roll_lanes(rows[y], 48 * y % 128) for y in range(8)]
    left, right = [], []
    for tile in range(3):
        a = c = None
        for y in range(8):
            lo, hi = max(48 * y, tile * 128), min(48 * y + 48, tile * 128 + 128)
            if lo >= hi:
                continue
            if a is None:
                a = c = placed[y]
            else:
                a = jnp.where(lane < lo - tile * 128, a, placed[y])
                c = jnp.where(turned_lane < lo - tile * 128, c, placed[y])
        left.append(a)
        right.append(roll_lanes(c, 64))
    return left, right


def three_terms(v):
    parts = []
    for _ in range(3):
        part = v.astype(BF16).astype(F32)
        parts.append(part)
        v = v - part
    return parts


def invert_factor(r, out):
    lane = lax.broadcasted_iota(jnp.int32, (8, 128), 1)
    sub = lax.broadcasted_iota(jnp.int32, (8, 128), 0)
    splat = lambda v, i, j: jnp.broadcast_to(v[i:i + 1, j:j + 1], (8, 128))
    spread = lambda v, i: jnp.broadcast_to(v[i:i + 1], (8, 128))

    def body(first_row, k):
        rows = pl.ds(pl.multiple_of(8 * k, 8), 8)
        top = [r[rows, 0:128], r[rows, 128:256]]
        off = 8 * lax.rem(k, 16)
        block = pltpu.roll(jnp.where(k >= 16, top[1], top[0]), lax.rem(128 - off, 128), 1)
        s = {(i, j): splat(block, j, i) for i in range(8) for j in range(i + 1)}
        recip, low = [], {}
        for col in range(8):
            recip.append(1.0 / s[col, col])
            for i in range(col + 1, 8):
                low[i, col] = s[i, col] * recip[col]
            for i in range(col + 1, 8):
                for j in range(col + 1, i + 1):
                    s[i, j] = s[i, j] - low[i, col] * s[j, col]
        inv = {}
        for j in range(8):
            for i in range(j + 1, 8):
                t = low[i, j]
                for p in range(j + 1, i):
                    t = t + low[i, p] * inv[p, j]
                inv[i, j] = -t
        cols, cols_t = [], []
        for j in range(8):
            v = jnp.where(sub == j, 1.0, 0.0)
            for i in range(j + 1, 8):
                v = jnp.where(sub == i, inv[i, j], v)
            cols.append(v)
            w = jnp.where(sub == j, 1.0, 0.0)
            for i in range(j):
                w = jnp.where(sub == i, inv[j, i], w)
            cols_t.append(w)
        pivot = recip[0]
        for i in range(1, 8):
            pivot = jnp.where(sub == i, recip[i], pivot)
        zs, ss = [], []
        for t in range(2):
            local = lane + 128 * t - 8 * k
            inside = jnp.logical_and(local >= 0, local < 8)
            v = jnp.where(inside, jnp.where(local == sub, 1.0, 0.0), top[t])
            y = cols[0] * spread(v, 0)
            for j in range(1, 8):
                y = y + cols[j] * spread(v, j)
            out[rows, 128 * t:128 * t + 128] = jnp.where(local < 8, y * jnp.sqrt(pivot), 0.0)
            y = y * pivot
            z = cols_t[0] * spread(y, 0)
            for j in range(1, 8):
                z = z + cols_t[j] * spread(y, j)
            zs.append(z)
            ss.append(jnp.where(local < 8, 0.0, top[t]))
        z, w = three_terms(jnp.concatenate(zs, 1)), three_terms(jnp.concatenate(ss, 1))
        left = jnp.concatenate([w[0], w[0], w[1], w[0], w[1], w[2]], 0).astype(BF16)
        right = jnp.concatenate([z[0], z[1], z[0], z[2], z[1], z[0]], 0).astype(BF16)
        live = slice(8 * first_row, M)
        update = lax.dot_general(left[:, live], right, (((0,), (0,)), ((), ())),
                                 preferred_element_type=F32)
        local = lax.broadcasted_iota(jnp.int32, (M - 8 * first_row, 256), 1) - 8 * k
        inside = jnp.logical_and(local >= 0, local < 8)
        r[live, :] = jnp.where(inside, 0.0, r[live, :]) - update

    for part in range(3):
        def segment(k, c):
            body(8 * part, k)
            return c
        lax.fori_loop(8 * part, 8 * part + 8, segment, 0)


def kernel(x_ref, p_ref, w_hbm, c_hbm, out_ref, recv, pot_in, w_ref, c_ref, field_a, field_b, pot, pack,
           own, part, rs_buf, xy_buf, sums, gsum, packed, work, inv_ref, rot, send_sems, recv_sems):
    b = lax.axis_index("band")
    d = lax.axis_index("dom")
    core = lax.rem(b, 2)
    y_pos, zh, x_pos = d // 8, lax.rem(d // 4, 2), lax.rem(d, 4)
    two = lax.rem(core + d, 2) == 0
    first = 3 * (d // 2) + lax.rem(d, 2) * (2 - core)
    me = d * 4 + b
    partner = b + 1 - 2 * core

    def remote(src, dst, send, receive, to_b, to_d):
        pltpu.make_async_remote_copy(
            src_ref=src, dst_ref=dst, send_sem=send_sems.at[send], recv_sem=recv_sems.at[receive],
            device_id=(to_b, to_d), device_id_type=MESH).start()

    def local(src, dst, receive):
        pltpu.make_async_copy(src, dst, recv_sems.at[receive]).start()

    def arrived(ref, receive):
        pltpu.make_async_copy(ref, ref, recv_sems.at[receive]).wait()

    barrier = pltpu.get_barrier_semaphore()

    def greet(i, c):
        to = lax.rem(me + i, 128)
        pl.semaphore_signal(barrier, inc=1, device_id=(lax.rem(to, 4), to // 4), device_id_type=MESH)
        return c

    lax.fori_loop(1, 128, greet, 0)
    pl.semaphore_wait(barrier, 127)

    def send_orbital(i, c):
        o = lax.rem(first + 2 + i, 48)
        r = lax.rem(o, 3)
        to = 2 * (o // 3) + jnp.where(r >= 2 - core, 1, 0)
        slot = jnp.where(r == 1 + core, 1, 0)
        src = x_ref.at[:, o, :]
        dst = recv.at[slot, lax.rem(d, 4), :, d // 4, :]

        @pl.when(to == d)
        def _():
            local(src, dst, slot)

        @pl.when(to != d)
        def _():
            remote(src, dst, 0, slot, b, to)
        return c

    lax.fori_loop(0, 48, send_orbital, 0)
    half = p_ref.at[:, pl.ds(pl.multiple_of(1152 * core, 128), 1152)]
    half_dst = pot_in.at[core, lax.rem(d, 4), :, d // 4, :]
    local(half, half_dst, 2)

    def send_potential(i, c):
        remote(half, half_dst, 1, 2, b, lax.rem(d + i, 32))
        return c

    lax.fori_loop(1, 32, send_potential, 0)
    local(w_hbm, w_ref, 12)
    local(c_hbm, c_ref, 13)

    @pl.when(jnp.logical_not(two))
    def _():
        recv[1] = jnp.zeros_like(recv[1])

    arrived(recv.at[0], 0)

    @pl.when(two)
    def _():
        arrived(recv.at[1], 1)

    arrived(w_ref, 12)
    arrived(c_ref, 13)

    def unpack(n, c):
        yb, q = n // 4, lax.rem(n, 4)
        lanes = [pl.ds(pl.multiple_of(yb * 384 + 128 * t, 128), 128) for t in range(3)]
        for j in range(3):
            rows = to_rows([recv[0, q, j, :, s] for s in lanes], [recv[1, q, j, :, s] for s in lanes])
            for y in range(8):
                field_a[yb * 8 + y, pl.ds(pl.multiple_of(q * 24 + 8 * j, 8), 8), :] = rows[y]
        return c

    lax.fori_loop(0, 24, unpack, 0)

    def step(src, dst, begin, end, is_first):
        def block(n, c):
            y0 = n * ROWS
            values = src[pl.ds(y0, ROWS)].reshape(ROWS * 96, 128)
            high = values.astype(BF16)
            low = (values - high.astype(F32)).astype(BF16)
            along_z = jnp.dot(jnp.concatenate([high, low], 1), w_ref[...], preferred_element_type=F32)
            along_x = []
            for r in range(0, ROWS, 2):
                one, other = slice(96 * r, 96 * r + 96), slice(96 * r + 96, 96 * r + 192)
                columns = jnp.concatenate([jnp.concatenate([high[one], high[other]], 1),
                                           jnp.concatenate([low[one], low[other]], 1)], 0)
                along_x.append(jnp.dot(c_ref[...], columns, preferred_element_type=F32))
            at = [lax.rem(y0 + 48 + s, 48) for s in range(-6, ROWS + 6)]
            for r in range(ROWS):
                for i in range(12):
                    rows = pl.ds(8 * i, 8)
                    centre = src[y0 + r, rows, :]
                    acc = centre * (DIAGONAL if is_first else pot[y0 + r, rows, :])
                    for k in range(1, 7):
                        acc = acc + COEFS[k] * (src[at[6 + r + k], rows, :] + src[at[6 + r - k], rows, :])
                    z = along_z[96 * r + 8 * i:96 * r + 8 * i + 8]
                    half_lanes = slice(128 * (r % 2), 128 * (r % 2) + 128)
                    x = (along_x[r // 2][8 * i:8 * i + 8, half_lanes]
                         + along_x[r // 2][96 + 8 * i:96 + 8 * i + 8, half_lanes])
                    acc = acc + ((z[:, :128] + z[:, 128:]) + x)
                    dst[y0 + r, rows, :] = 0.5 * acc if is_first else acc - dst[y0 + r, rows, :]
            return c

        lax.fori_loop(begin, end, block, 0)

    step(field_a, field_b, 0, 4, True)
    arrived(pot_in.at[core], 2)
    remote(pot_in.at[core], pot_in.at[core], 7, 11, partner, d)
    step(field_a, field_b, 4, 6, True)
    arrived(pot_in.at[core], 11)

    def unpack_potential(n, c):
        yb, q = n // 4, lax.rem(n, 4)
        lanes = [pl.ds(pl.multiple_of(lax.rem(yb, 3) * 384 + 128 * t, 128), 128) for t in range(3)]
        for j in range(3):
            planes = [pot_in[yb // 3, q, j, :, s] for s in lanes]
            rows = to_rows(planes, planes)
            for y in range(8):
                here = pl.ds(pl.multiple_of(q * 24 + 8 * j, 8), 8)
                v = SCALE * rows[y]
                pot[yb * 8 + y, here, :] = v + DIAGONAL
                field_b[yb * 8 + y, here, :] = field_b[yb * 8 + y, here, :] + (0.5 * v) * field_a[yb * 8 + y, here, :]
        return c

    lax.fori_loop(0, 24, unpack_potential, 0)
    step(field_b, field_a, 0, 6, False)
    step(field_a, field_b, 0, 6, False)
    step(field_b, field_a, 0, 6, False)

    def repack(n, c):
        yb, q = n // 4, lax.rem(n, 4)
        for j in range(3):
            rows = [field_a[yb * 8 + y, pl.ds(pl.multiple_of(q * 24 + 8 * j, 8), 8), :] for y in range(8)]
            left, right = to_tiles(rows)
            for t in range(3):
                pack[q, j * 18 + yb * 3 + t, 0] = left[t]
                pack[q, j * 18 + yb * 3 + t, 1] = right[t]
        return c

    lax.fori_loop(0, 24, repack, 0)

    def quarter(band):
        return 14 * band - jnp.maximum(band - 1, 0)

    def spread(count):
        def send(i, c):
            to = lax.rem(me + i, 128)
            to_b, to_d = lax.rem(to, 4), to // 4
            src = pack.at[lax.rem(to_d, 4), pl.ds(quarter(to_b), TILES), pl.ds(0, count), to_d // 4, :]
            remote(src, own.at[:, pl.ds(48 * b + first, count), :], 2, 3, to_b, to_d)
            return c

        lax.fori_loop(1, 128, send, 0)
        local(pack.at[lax.rem(d, 4), pl.ds(quarter(b), TILES), pl.ds(0, count), d // 4, :],
              own.at[:, pl.ds(48 * b + first, count), :], 3)

    @pl.when(two)
    def _():
        spread(2)

    @pl.when(jnp.logical_not(two))
    def _():
        spread(1)

    arrived(own, 3)

    total = jnp.zeros((M, M), F32)
    for i in range(0, TILES, 2):
        one = own[i]
        if i == 0:
            one = jnp.where(b >= 2, 0.0, one)
        both = jnp.concatenate([one, own[i + 1]], 1)
        total = total + lax.dot_general(both, both, (((1,), (1,)), ((), ())), precision=lax.Precision.HIGHEST,
                                        preferred_element_type=F32)
    near = total[:, :128]
    far = jnp.concatenate([total[:, 128:], jnp.zeros((M, 64), F32)], 1)
    left_half = lax.broadcasted_iota(jnp.int32, (64, 128), 1) < 64
    packed[0:64] = near[0:64]
    packed[64:128] = jnp.where(left_half, far[0:64], near[64:128])
    packed[128:192] = jnp.where(left_half, far[64:128], pltpu.roll(far[128:192], 64, 1))
    for i in range(8):
        part[i] = packed[24 * i:24 * i + 24]

    mine = zh * 4 + b
    for i in range(1, 8):
        to = lax.rem(mine + i, 8)
        remote(part.at[to], rs_buf.at[mine], 4, 4, lax.rem(to, 4), y_pos * 8 + (to // 4) * 4 + x_pos)
    rs_buf[mine] = part[mine]
    arrived(rs_buf.at[pl.ds(0, 7)], 4)
    acc = rs_buf[0]
    for i in range(1, 8):
        acc = acc + rs_buf[i]
    sums[...] = acc
    spot = y_pos * 4 + x_pos
    for i in range(1, 16):
        to = lax.rem(spot + i, 16)
        remote(sums, xy_buf.at[spot], 5, 5, b, (to // 4) * 8 + zh * 4 + lax.rem(to, 4))
    xy_buf[spot] = acc
    arrived(xy_buf.at[pl.ds(0, 15)], 5)
    acc = xy_buf[0]
    for i in range(1, 16):
        acc = acc + xy_buf[i]
    acc = acc / CELLS
    gsum[mine] = acc
    for i in range(1, 8):
        to = lax.rem(mine + i, 8)
        remote(gsum.at[mine], gsum.at[mine], 6, 6, lax.rem(to, 4), y_pos * 8 + (to // 4) * 4 + x_pos)
    arrived(gsum.at[pl.ds(0, 7)], 6)

    for i in range(8):
        packed[24 * i:24 * i + 24] = gsum[i]
    work[0:64, 0:128] = packed[0:64]
    work[0:64, 128:256] = packed[64:128]
    work[64:128, 0:128] = packed[64:128]
    work[64:128, 128:256] = packed[128:192]
    work[128:192, 0:128] = packed[128:192]
    work[128:192, 128:256] = pltpu.roll(packed[128:192], 64, 1)
    invert_factor(work, inv_ref)

    def rotate(n, c):
        columns = jnp.concatenate([own[2 * n], own[2 * n + 1]], 1)
        product = jnp.dot(inv_ref[:, 0:M], columns, precision=lax.Precision.HIGHEST, preferred_element_type=F32)
        for i in range(2):
            tile = quarter(b) + 2 * n + i
            place = out_ref.at[tile // 18, :, pl.ds(pl.multiple_of(128 * lax.rem(tile, 18), 128), 128)]
            for band in range(4):
                rot[2 * n + i, band] = product[48 * band:48 * band + 48, 128 * i:128 * i + 128]

            @pl.when(jnp.logical_or(b < 2, 2 * n + i > 0))
            def _():
                for away in (2, 3, 1):
                    to = lax.rem(b + away, 4)
                    remote(rot.at[2 * n + i, to], place, 8, 7 + b, to, d)
                local(rot.at[2 * n + i, b], place, 7 + b)
        return c

    lax.fori_loop(0, TILES // 2, rotate, 0)

    def drain(ref, sem, times):
        def body(i, c):
            pltpu.make_async_copy(ref, ref, sem).wait()
            return c
        lax.fori_loop(0, times, body, 0)

    tile = rot.at[0, 0]
    mine_tiles = jnp.where(b < 2, 14, 13)
    for band in range(4):
        arrived(rot.at[pl.ds(0, 14 if band < 2 else 13), 0], 7 + band)
    drain(tile, send_sems.at[8], 3 * mine_tiles)
    orbital = recv.at[0, 0, :, 0, :]
    drain(orbital, send_sems.at[0], jnp.where(two, 46, 47))
    drain(half_dst, send_sems.at[1], 31)
    drain(pot_in.at[0], send_sems.at[7], 1)
    share = pack.at[0, pl.ds(0, TILES), pl.ds(0, 1), 0, :]
    drain(share, send_sems.at[2], jnp.where(two, 254, 127))
    drain(sums, send_sems.at[4], 7)
    drain(sums, send_sems.at[5], 15)
    drain(sums, send_sems.at[6], 7)


def per_device(orbitals, potential):
    anywhere = pl.BlockSpec(memory_space=pl.ANY)
    out = pl.pallas_call(
        kernel,
        out_shape=jax.ShapeDtypeStruct((3, 48, 2304), F32),
        in_specs=[anywhere] * 4,
        out_specs=pl.BlockSpec(memory_space=pltpu.VMEM),
        scratch_shapes=[
            pltpu.VMEM((2, 4, 3, 8, 2304), F32),
            pltpu.VMEM((2, 4, 3, 8, 1152), F32),
            pltpu.VMEM((256, 256), BF16),
            pltpu.VMEM((192, 192), BF16),
            pltpu.VMEM((48, 96, 128), F32),
            pltpu.VMEM((48, 96, 128), F32),
            pltpu.VMEM((48, 96, 128), F32),
            pltpu.VMEM((4, 54, 2, 8, 128), F32),
            pltpu.VMEM((TILES, M, 128), F32),
            pltpu.VMEM((8, 24, 128), F32),
            pltpu.VMEM((8, 24, 128), F32),
            pltpu.VMEM((16, 24, 128), F32),
            pltpu.VMEM((24, 128), F32),
            pltpu.VMEM((8, 24, 128), F32),
            pltpu.VMEM((M, 128), F32),
            pltpu.VMEM((M, 256), F32),
            pltpu.VMEM((M, 256), F32),
            pltpu.VMEM((TILES, 4, 48, 128), F32),
            pltpu.SemaphoreType.DMA((9,)),
            pltpu.SemaphoreType.DMA((14,)),
        ],
        compiler_params=pltpu.CompilerParams(
            collective_id=0, has_side_effects=True, vmem_limit_bytes=56 * 2**20),
    )(jnp.transpose(orbitals, (1, 0, 2)), potential, jnp.asarray(z_matrix()), jnp.asarray(x_matrix()))
    return jnp.transpose(out, (1, 0, 2))


def solution(mesh):
    placed = (P("band", "dom", None), P("dom", None))
    return jax.shard_map(
        per_device, mesh=mesh, in_specs=placed, out_specs=P("band", "dom", None), check_vma=False
    )
```

time: 257 us -> 124 us (0.48)
  Pallas kernels: 189 us -> 121 us
  other arithmetic: 49.3 us -> 0 us
  local copies, waits for them, and re-layouts: 10.5 us -> 2.47 us
  matrix products: 6.39 us -> 0 us
    pallas_call x1, Pallas kernels: 189 us -> 121 us  [per_device(): pl.pallas_call(kernel, out_shape=jax.ShapeDtypeStruct((3, 48, 2304), F32)...]
    another operation x13 -> x0, other arithmetic: 48.6 us -> none  [the longest x7 28.8 us: per_device(): lower = jnp.linalg.cholesky(intersection)]
    squeeze x2 -> x0, local copies, waits for them, and re-layouts: 5.51 us -> none  [per_device(): everyone = jnp.concatenate([e[0], e[1], e[2, 1:], e[3, 1:]], 0)]
    dot_general x1 -> x0, matrix products: 5.08 us -> none  [per_device(): jnp.einsum('ij,tjc->tic', own, everyone, precision=lax.Precision.HIGHEST,...]
where the time goes in v2:
time: 124 us
  Pallas kernels  121 us (98%)
  local copies, waits for them, and re-layouts  2.47 us (2%)
    pallas_call x1, Pallas kernels, per_device(): pl.pallas_call(kernel, out_shape=jax.ShapeDtypeStruct((3, 48, 2304), F32)...  121 us

profile of v2, /device:TPU:1, one launch (start us, length us, event | category | flops | bytes accessed | tf_op | source)
XLA Modules:
  0.0 123.8 jit_solution(1078349576283328591)
XLA Ops:
  0.0 121.4 %shard_map.46 = f32[3,48,2304]{2,1,0:T(8,128)} custom-call(f32[3,48,2304]{2,1,0:T(8,128)} %bitcast.3, f32[3,2304]{1,0:T(4,128)} %p_ref.1, bf16[256,256]{1,0:T(8,128)(2,1)} %constant.4.clone.w_hbm, bf16[192,192]{1,0:T(8,128)(2,1)} %constant.5.clone.c_hbm), custom_call_target="tpu_custom_call" | custom-call | tf_op jit(solution)/shard_map/pallas_call | solution.py:461
  121.4 2.5 %copy.6 = f32[48,3,2304]{2,0,1:T(8,128)} copy(f32[48,3,2304]{2,0,1:T(8,128)} %bitcast.2) | data formatting | bytes 2654208

commit v3 on v2

--- a/solution.py
+++ b/solution.py
@@ -34,11 +34,11 @@
 
 def z_matrix():
     full = np.zeros((128, 128), np.float32)
-    for slot in range(2):
+    for half in range(2):
         for z in range(48):
             for k in range(1, 7):
-                full[slot * 64 + z, slot * 64 + (z + k) % 48] += COEFS[k]
-                full[slot * 64 + z, slot * 64 + (z - k) % 48] += COEFS[k]
+                full[half * 64 + z, half * 64 + (z + k) % 48] += COEFS[k]
+                full[half * 64 + z, half * 64 + (z - k) % 48] += COEFS[k]
     row = np.concatenate(two_terms(full), 1)
     return np.concatenate([row, row], 0)
 
@@ -84,7 +84,7 @@
 
 def to_tiles(rows):
     lane = lane_index()
-    turned_lane = lax.rem(lane + 64, 128)
+    turned_lane = jnp.where(lane < 64, lane + 64, lane - 64)
     placed = [roll_lanes(rows[y], 48 * y % 128) for y in range(8)]
     left, right = [], []
     for tile in range(3):
@@ -206,6 +206,12 @@
     def arrived(ref, receive):
         pltpu.make_async_copy(ref, ref, recv_sems.at[receive]).wait()
 
+    def drain(ref, sem, times):
+        def body(i, c):
+            pltpu.make_async_copy(ref, ref, sem).wait()
+            return c
+        lax.fori_loop(0, times, body, 0)
+
     barrier = pltpu.get_barrier_semaphore()
 
     def greet(i, c):
@@ -216,63 +222,85 @@
     lax.fori_loop(1, 128, greet, 0)
     pl.semaphore_wait(barrier, 127)
 
-    def send_orbital(i, c):
-        o = lax.rem(first + 2 + i, 48)
-        r = lax.rem(o, 3)
-        to = 2 * (o // 3) + jnp.where(r >= 2 - core, 1, 0)
-        slot = jnp.where(r == 1 + core, 1, 0)
-        src = x_ref.at[:, o, :]
-        dst = recv.at[slot, lax.rem(d, 4), :, d // 4, :]
-
-        @pl.when(to == d)
-        def _():
-            local(src, dst, slot)
-
-        @pl.when(to != d)
-        def _():
-            remote(src, dst, 0, slot, b, to)
-        return c
-
-    lax.fori_loop(0, 48, send_orbital, 0)
     half = p_ref.at[:, pl.ds(pl.multiple_of(1152 * core, 128), 1152)]
     half_dst = pot_in.at[core, lax.rem(d, 4), :, d // 4, :]
-    local(half, half_dst, 2)
 
     def send_potential(i, c):
         remote(half, half_dst, 1, 2, b, lax.rem(d + i, 32))
         return c
 
+    local(half, half_dst, 2)
     lax.fori_loop(1, 32, send_potential, 0)
+
+    def send_orbital(slot):
+        def send(i, c):
+            to = lax.rem(d + i, 32)
+            to_two = lax.rem(core + to, 2) == 0
+            o = 3 * (to // 2) + lax.rem(to, 2) * (2 - core) + slot
+            src = x_ref.at[:, o, :]
+            dst = recv.at[slot, lax.rem(d, 4), :, d // 4, :]
+
+            def start():
+                remote(src, dst, 0, slot, b, to)
+
+            if slot == 0:
+                start()
+            else:
+                pl.when(to_two)(start)
+            return c
+
+        def keep():
+            local(x_ref.at[:, first + slot, :], recv.at[slot, lax.rem(d, 4), :, d // 4, :], slot)
+
+        if slot == 0:
+            keep()
+        else:
+            pl.when(two)(keep)
+        lax.fori_loop(1, 32, send, 0)
+
+    send_orbital(0)
+    send_orbital(1)
     local(w_hbm, w_ref, 12)
     local(c_hbm, c_ref, 13)
 
-    @pl.when(jnp.logical_not(two))
-    def _():
-        recv[1] = jnp.zeros_like(recv[1])
-
-    arrived(recv.at[0], 0)
-
-    @pl.when(two)
-    def _():
-        arrived(recv.at[1], 1)
-
-    arrived(w_ref, 12)
-    arrived(c_ref, 13)
-
-    def unpack(n, c):
-        yb, q = n // 4, lax.rem(n, 4)
-        lanes = [pl.ds(pl.multiple_of(yb * 384 + 128 * t, 128), 128) for t in range(3)]
-        for j in range(3):
-            rows = to_rows([recv[0, q, j, :, s] for s in lanes], [recv[1, q, j, :, s] for s in lanes])
-            for y in range(8):
-                field_a[yb * 8 + y, pl.ds(pl.multiple_of(q * 24 + 8 * j, 8), 8), :] = rows[y]
-        return c
-
-    lax.fori_loop(0, 24, unpack, 0)
-
-    def step(src, dst, begin, end, is_first):
+    def unpack(load, store):
+        def body(n, c):
+            yb, q = n // 4, lax.rem(n, 4)
+            for j in range(3):
+                rows = to_rows(load(0, yb, q, j), load(1, yb, q, j))
+                for y in range(8):
+                    store(yb * 8 + y, pl.ds(pl.multiple_of(q * 24 + 8 * j, 8), 8), rows[y])
+            return c
+
+        lax.fori_loop(0, 12, body, 0)
+
+    def chunk(start, t):
+        return pl.ds(pl.multiple_of(start + 128 * t, 128), 128)
+
+    def load_potential(side, yb, q, j):
+        return [pot_in[side, q, j, :, chunk(yb * 384, t)] for t in range(3)]
+
+    def store_potential(y, rows, v):
+        pot[y, rows, :] = SCALE * v + DIAGONAL
+
+    arrived(pot_in.at[core], 2)
+    remote(pot_in.at[core], pot_in.at[core], 7, 11, partner, d)
+    arrived(pot_in.at[core], 11)
+    unpack(load_potential, store_potential)
+
+    def halo(field):
+        def body(i, c):
+            for r in range(12):
+                rows = pl.ds(8 * r, 8)
+                field[30 + i, rows, :] = pltpu.roll(field[6 + i, rows, :], 64, 1)
+                field[i, rows, :] = pltpu.roll(field[24 + i, rows, :], 64, 1)
+            return c
+
+        lax.fori_loop(0, 6, body, 0)
+
+    def step(src, dst, is_first):
         def block(n, c):
-            y0 = n * ROWS
+            y0 = n * ROWS + 6
             values = src[pl.ds(y0, ROWS)].reshape(ROWS * 96, 128)
             high = values.astype(BF16)
             low = (values - high.astype(F32)).astype(BF16)
@@ -283,14 +311,12 @@
                 columns = jnp.concatenate([jnp.concatenate([high[one], high[other]], 1),
                                            jnp.concatenate([low[one], low[other]], 1)], 0)
                 along_x.append(jnp.dot(c_ref[...], columns, preferred_element_type=F32))
-            at = [lax.rem(y0 + 48 + s, 48) for s in range(-6, ROWS + 6)]
             for r in range(ROWS):
                 for i in range(12):
                     rows = pl.ds(8 * i, 8)
-                    centre = src[y0 + r, rows, :]
-                    acc = centre * (DIAGONAL if is_first else pot[y0 + r, rows, :])
+                    acc = src[y0 + r, rows, :] * pot[y0 + r - 6, rows, :]
                     for k in range(1, 7):
-                        acc = acc + COEFS[k] * (src[at[6 + r + k], rows, :] + src[at[6 + r - k], rows, :])
+                        acc = acc + COEFS[k] * (src[y0 + r + k, rows, :] + src[y0 + r - k, rows, :])
                     z = along_z[96 * r + 8 * i:96 * r + 8 * i + 8]
                     half_lanes = slice(128 * (r % 2), 128 * (r % 2) + 128)
                     x = (along_x[r // 2][8 * i:8 * i + 8, half_lanes]
@@ -299,67 +325,57 @@
                     dst[y0 + r, rows, :] = 0.5 * acc if is_first else acc - dst[y0 + r, rows, :]
             return c
 
-        lax.fori_loop(begin, end, block, 0)
-
-    step(field_a, field_b, 0, 4, True)
-    arrived(pot_in.at[core], 2)
-    remote(pot_in.at[core], pot_in.at[core], 7, 11, partner, d)
-    step(field_a, field_b, 4, 6, True)
-    arrived(pot_in.at[core], 11)
-
-    def unpack_potential(n, c):
-        yb, q = n // 4, lax.rem(n, 4)
-        lanes = [pl.ds(pl.multiple_of(lax.rem(yb, 3) * 384 + 128 * t, 128), 128) for t in range(3)]
-        for j in range(3):
-            planes = [pot_in[yb // 3, q, j, :, s] for s in lanes]
-            rows = to_rows(planes, planes)
-            for y in range(8):
-                here = pl.ds(pl.multiple_of(q * 24 + 8 * j, 8), 8)
-                v = SCALE * rows[y]
-                pot[yb * 8 + y, here, :] = v + DIAGONAL
-                field_b[yb * 8 + y, here, :] = field_b[yb * 8 + y, here, :] + (0.5 * v) * field_a[yb * 8 + y, here, :]
-        return c
-
-    lax.fori_loop(0, 24, unpack_potential, 0)
-    step(field_b, field_a, 0, 6, False)
-    step(field_a, field_b, 0, 6, False)
-    step(field_b, field_a, 0, 6, False)
-
-    def repack(n, c):
-        yb, q = n // 4, lax.rem(n, 4)
-        for j in range(3):
-            rows = [field_a[yb * 8 + y, pl.ds(pl.multiple_of(q * 24 + 8 * j, 8), 8), :] for y in range(8)]
-            left, right = to_tiles(rows)
-            for t in range(3):
-                pack[q, j * 18 + yb * 3 + t, 0] = left[t]
-                pack[q, j * 18 + yb * 3 + t, 1] = right[t]
-        return c
-
-    lax.fori_loop(0, 24, repack, 0)
+        lax.fori_loop(0, 24 // ROWS, block, 0)
 
     def quarter(band):
         return 14 * band - jnp.maximum(band - 1, 0)
 
-    def spread(count):
+    def spread(slot):
         def send(i, c):
             to = lax.rem(me + i, 128)
             to_b, to_d = lax.rem(to, 4), to // 4
-            src = pack.at[lax.rem(to_d, 4), pl.ds(quarter(to_b), TILES), pl.ds(0, count), to_d // 4, :]
-            remote(src, own.at[:, pl.ds(48 * b + first, count), :], 2, 3, to_b, to_d)
+            src = pack.at[slot, lax.rem(to_d, 4), pl.ds(quarter(to_b), TILES), to_d // 4, :]
+            remote(src, own.at[:, 48 * b + first + slot, :], 2, 3, to_b, to_d)
             return c
 
         lax.fori_loop(1, 128, send, 0)
-        local(pack.at[lax.rem(d, 4), pl.ds(quarter(b), TILES), pl.ds(0, count), d // 4, :],
-              own.at[:, pl.ds(48 * b + first, count), :], 3)
-
-    @pl.when(two)
-    def _():
-        spread(2)
-
-    @pl.when(jnp.logical_not(two))
-    def _():
-        spread(1)
-
+        local(pack.at[slot, lax.rem(d, 4), pl.ds(quarter(b), TILES), d // 4, :],
+              own.at[:, 48 * b + first + slot, :], 3)
+
+    def filter_orbital(slot):
+        def load(side, yb, q, j):
+            return [recv[slot, q, j, :, chunk(yb * 384 + 1152 * side, t)] for t in range(3)]
+
+        def store(y, rows, v):
+            field_a[y + 6, rows, :] = v
+
+        def repack(n, c):
+            yb, q = n // 4, lax.rem(n, 4)
+            for j in range(3):
+                rows = [field_a[6 + yb * 8 + y, pl.ds(pl.multiple_of(q * 24 + 8 * j, 8), 8), :] for y in range(8)]
+                left, right = to_tiles(rows)
+                for t in range(3):
+                    pack[slot, q, j * 18 + yb * 3 + t] = left[t]
+                    pack[slot, q, j * 18 + 9 + yb * 3 + t] = right[t]
+            return c
+
+        arrived(recv.at[slot], slot)
+        unpack(load, store)
+        halo(field_a)
+        step(field_a, field_b, True)
+        halo(field_b)
+        step(field_b, field_a, False)
+        halo(field_a)
+        step(field_a, field_b, False)
+        halo(field_b)
+        step(field_b, field_a, False)
+        lax.fori_loop(0, 12, repack, 0)
+        spread(slot)
+
+    arrived(w_ref, 12)
+    arrived(c_ref, 13)
+    filter_orbital(0)
+    pl.when(two)(lambda: filter_orbital(1))
     arrived(own, 3)
 
     total = jnp.zeros((M, M), F32)
@@ -434,12 +450,6 @@
 
     lax.fori_loop(0, TILES // 2, rotate, 0)
 
-    def drain(ref, sem, times):
-        def body(i, c):
-            pltpu.make_async_copy(ref, ref, sem).wait()
-            return c
-        lax.fori_loop(0, times, body, 0)
-
     tile = rot.at[0, 0]
     mine_tiles = jnp.where(b < 2, 14, 13)
     for band in range(4):
@@ -449,7 +459,7 @@
     drain(orbital, send_sems.at[0], jnp.where(two, 46, 47))
     drain(half_dst, send_sems.at[1], 31)
     drain(pot_in.at[0], send_sems.at[7], 1)
-    share = pack.at[0, pl.ds(0, TILES), pl.ds(0, 1), 0, :]
+    share = pack.at[0, 0, pl.ds(0, TILES), 0, :]
     drain(share, send_sems.at[2], jnp.where(two, 254, 127))
     drain(sums, send_sems.at[4], 7)
     drain(sums, send_sems.at[5], 15)
@@ -468,10 +478,10 @@
             pltpu.VMEM((2, 4, 3, 8, 1152), F32),
             pltpu.VMEM((256, 256), BF16),
             pltpu.VMEM((192, 192), BF16),
-            pltpu.VMEM((48, 96, 128), F32),
-            pltpu.VMEM((48, 96, 128), F32),
-            pltpu.VMEM((48, 96, 128), F32),
-            pltpu.VMEM((4, 54, 2, 8, 128), F32),
+            pltpu.VMEM((36, 96, 128), F32),
+            pltpu.VMEM((36, 96, 128), F32),
+            pltpu.VMEM((24, 96, 128), F32),
+            pltpu.VMEM((2, 4, 54, 8, 128), F32),
             pltpu.VMEM((TILES, M, 128), F32),
             pltpu.VMEM((8, 24, 128), F32),
             pltpu.VMEM((8, 24, 128), F32),

time: 124 us -> 114 us (0.919)
  Pallas kernels: 121 us -> 111 us
    pallas_call x1, Pallas kernels: 121 us -> 111 us  [per_device(): pl.pallas_call(kernel, out_shape=jax.ShapeDtypeStruct((3, 48, 2304), F32)...]
where the time goes in v3:
time: 114 us
  Pallas kernels  111 us (97%)
  local copies, waits for them, and re-layouts  2.47 us (2%)
    pallas_call x1, Pallas kernels, per_device(): pl.pallas_call(kernel, out_shape=jax.ShapeDtypeStruct((3, 48, 2304), F32)...  111 us
    unnamed x1, local copies, waits for them, and re-layouts  2.47 us

profile of v3, /device:TPU:1, one launch (start us, length us, event | category | flops | bytes accessed | tf_op | source)
XLA Modules:
  0.0 113.8 jit_solution(2481623884518702349)
XLA Ops:
  0.0 111.3 %shard_map.46 = f32[3,48,2304]{2,1,0:T(8,128)} custom-call(f32[3,48,2304]{2,1,0:T(8,128)} %bitcast.3, f32[3,2304]{1,0:T(4,128)} %p_ref.1, bf16[256,256]{1,0:T(8,128)(2,1)} %constant.4.clone.w_hbm, bf16[192,192]{1,0:T(8,128)(2,1)} %constant.5.clone.c_hbm), custom_call_target="tpu_custom_call" | custom-call | tf_op jit(solution)/shard_map/pallas_call | solution.py:471
  111.3 2.5 %copy.6 = f32[48,3,2304]{2,0,1:T(8,128)} copy(f32[48,3,2304]{2,0,1:T(8,128)} %bitcast.2) | data formatting | bytes 2654208

commit v4 on v3

--- a/solution.py
+++ b/solution.py
@@ -24,6 +24,7 @@
 COEFS = [-0.5 * SCALE * w for w in stencil_weights]
 DIAGONAL = 3.0 * COEFS[0] - 7.0 * SCALE
 TILES = 14
+EARLY = 8
 ROWS = 8
 
 
@@ -185,7 +186,7 @@
 
 
 def kernel(x_ref, p_ref, w_hbm, c_hbm, out_ref, recv, pot_in, w_ref, c_ref, field_a, field_b, pot, pack,
-           own, part, rs_buf, xy_buf, sums, gsum, packed, work, inv_ref, rot, send_sems, recv_sems):
+           own, part, rs_buf, xy_buf, sums, gsum, packed, work, inv_ref, rot, gathered, send_sems, recv_sems, ready):
     b = lax.axis_index("band")
     d = lax.axis_index("dom")
     core = lax.rem(b, 2)
@@ -215,12 +216,17 @@
     barrier = pltpu.get_barrier_semaphore()
 
     def greet(i, c):
-        to = lax.rem(me + i, 128)
-        pl.semaphore_signal(barrier, inc=1, device_id=(lax.rem(to, 4), to // 4), device_id_type=MESH)
+        pl.semaphore_signal(barrier, inc=1, device_id=(b, lax.rem(d + i, 32)), device_id_type=MESH)
         return c
 
-    lax.fori_loop(1, 128, greet, 0)
-    pl.semaphore_wait(barrier, 127)
+    def greet_again(i, c):
+        pl.semaphore_signal(ready, inc=1, device_id=(b, lax.rem(d + i, 32)), device_id_type=MESH)
+        return c
+
+    lax.fori_loop(1, 32, greet, 0)
+    for i in range(1, 4):
+        pl.semaphore_signal(barrier, inc=1, device_id=(lax.rem(b + i, 4), d), device_id_type=MESH)
+    pl.semaphore_wait(barrier, 34)
 
     half = p_ref.at[:, pl.ds(pl.multiple_of(1152 * core, 128), 1152)]
     half_dst = pot_in.at[core, lax.rem(d, 4), :, d // 4, :]
@@ -228,9 +234,6 @@
     def send_potential(i, c):
         remote(half, half_dst, 1, 2, b, lax.rem(d + i, 32))
         return c
-
-    local(half, half_dst, 2)
-    lax.fori_loop(1, 32, send_potential, 0)
 
     def send_orbital(slot):
         def send(i, c):
@@ -259,9 +262,12 @@
         lax.fori_loop(1, 32, send, 0)
 
     send_orbital(0)
-    send_orbital(1)
+    local(half, half_dst, 2)
+    lax.fori_loop(1, 32, send_potential, 0)
+    lax.fori_loop(1, 32, greet_again, 0)
     local(w_hbm, w_ref, 12)
     local(c_hbm, c_ref, 13)
+    pot[...] = jnp.full(pot.shape, DIAGONAL, F32)
 
     def unpack(load, store):
         def body(n, c):
@@ -280,27 +286,18 @@
     def load_potential(side, yb, q, j):
         return [pot_in[side, q, j, :, chunk(yb * 384, t)] for t in range(3)]
 
+    def put(field, y, rows, v):
+        field[y, rows, :] = v
+        field[24 + y, rows, :] = pltpu.roll(v, 64, 1)
+
     def store_potential(y, rows, v):
-        pot[y, rows, :] = SCALE * v + DIAGONAL
-
-    arrived(pot_in.at[core], 2)
-    remote(pot_in.at[core], pot_in.at[core], 7, 11, partner, d)
-    arrived(pot_in.at[core], 11)
-    unpack(load_potential, store_potential)
-
-    def halo(field):
-        def body(i, c):
-            for r in range(12):
-                rows = pl.ds(8 * r, 8)
-                field[30 + i, rows, :] = pltpu.roll(field[6 + i, rows, :], 64, 1)
-                field[i, rows, :] = pltpu.roll(field[24 + i, rows, :], 64, 1)
-            return c
-
-        lax.fori_loop(0, 6, body, 0)
-
-    def step(src, dst, is_first):
+        v = SCALE * v
+        pot[y, rows, :] = v + DIAGONAL
+        put(field_b, y, rows, field_b[y, rows, :] + (0.5 * v) * field_a[y, rows, :])
+
+    def step(src, dst, weight):
         def block(n, c):
-            y0 = n * ROWS + 6
+            y0 = n * ROWS
             values = src[pl.ds(y0, ROWS)].reshape(ROWS * 96, 128)
             high = values.astype(BF16)
             low = (values - high.astype(F32)).astype(BF16)
@@ -311,18 +308,20 @@
                 columns = jnp.concatenate([jnp.concatenate([high[one], high[other]], 1),
                                            jnp.concatenate([low[one], low[other]], 1)], 0)
                 along_x.append(jnp.dot(c_ref[...], columns, preferred_element_type=F32))
-            for r in range(ROWS):
-                for i in range(12):
-                    rows = pl.ds(8 * i, 8)
-                    acc = src[y0 + r, rows, :] * pot[y0 + r - 6, rows, :]
+            at = [lax.rem(y0 + 48 + s, 48) for s in range(-6, ROWS + 6)]
+            for i in range(12):
+                rows = pl.ds(8 * i, 8)
+                near = [src[y, rows, :] for y in at]
+                for r in range(ROWS):
+                    acc = near[6 + r] * pot[y0 + r, rows, :]
                     for k in range(1, 7):
-                        acc = acc + COEFS[k] * (src[y0 + r + k, rows, :] + src[y0 + r - k, rows, :])
+                        acc = acc + COEFS[k] * (near[6 + r + k] + near[6 + r - k])
                     z = along_z[96 * r + 8 * i:96 * r + 8 * i + 8]
                     half_lanes = slice(128 * (r % 2), 128 * (r % 2) + 128)
                     x = (along_x[r // 2][8 * i:8 * i + 8, half_lanes]
                          + along_x[r // 2][96 + 8 * i:96 + 8 * i + 8, half_lanes])
                     acc = acc + ((z[:, :128] + z[:, 128:]) + x)
-                    dst[y0 + r, rows, :] = 0.5 * acc if is_first else acc - dst[y0 + r, rows, :]
+                    put(dst, y0 + r, rows, weight * acc - dst[y0 + r, rows, :])
             return c
 
         lax.fori_loop(0, 24 // ROWS, block, 0)
@@ -342,17 +341,27 @@
         local(pack.at[slot, lax.rem(d, 4), pl.ds(quarter(b), TILES), d // 4, :],
               own.at[:, 48 * b + first + slot, :], 3)
 
-    def filter_orbital(slot):
+    def add_potential():
+        arrived(pot_in.at[core], 2)
+        remote(pot_in.at[core], pot_in.at[core], 7, 11, partner, d)
+        arrived(pot_in.at[core], 11)
+        unpack(load_potential, store_potential)
+
+    def send_second():
+        send_orbital(1)
+
+    def filter_orbital(slot, c):
         def load(side, yb, q, j):
             return [recv[slot, q, j, :, chunk(yb * 384 + 1152 * side, t)] for t in range(3)]
 
         def store(y, rows, v):
-            field_a[y + 6, rows, :] = v
+            put(field_a, y, rows, v)
+            field_b[y, rows, :] = jnp.zeros_like(v)
 
         def repack(n, c):
             yb, q = n // 4, lax.rem(n, 4)
             for j in range(3):
-                rows = [field_a[6 + yb * 8 + y, pl.ds(pl.multiple_of(q * 24 + 8 * j, 8), 8), :] for y in range(8)]
+                rows = [field_a[yb * 8 + y, pl.ds(pl.multiple_of(q * 24 + 8 * j, 8), 8), :] for y in range(8)]
                 left, right = to_tiles(rows)
                 for t in range(3):
                     pack[slot, q, j * 18 + yb * 3 + t] = left[t]
@@ -360,23 +369,42 @@
             return c
 
         arrived(recv.at[slot], slot)
+        pl.when(slot == 0)(send_second)
         unpack(load, store)
-        halo(field_a)
-        step(field_a, field_b, True)
-        halo(field_b)
-        step(field_b, field_a, False)
-        halo(field_a)
-        step(field_a, field_b, False)
-        halo(field_b)
-        step(field_b, field_a, False)
+
+        def steps(t, c):
+            step(field_a, field_b, jnp.where(t == 0, 0.5, 1.0))
+            pl.when(jnp.logical_and(slot == 0, t == 0))(add_potential)
+            step(field_b, field_a, 1.0)
+            return c
+
+        lax.fori_loop(0, 2, steps, 0)
+
+        @pl.when(slot == 0)
+        def _():
+            pl.semaphore_wait(ready, 31)
+
         lax.fori_loop(0, 12, repack, 0)
         spread(slot)
+        return c
 
     arrived(w_ref, 12)
     arrived(c_ref, 13)
-    filter_orbital(0)
-    pl.when(two)(lambda: filter_orbital(1))
+    lax.fori_loop(0, jnp.where(two, 2, 1), filter_orbital, 0)
     arrived(own, 3)
+
+    z_peer = lax.rem(b + 2, 4)
+    other = lax.rem(partner + 2, 4)
+    PART = EARLY // 2
+
+    def exchange(i):
+        tiles = pl.ds(PART * i, PART)
+        remote(own.at[tiles], gathered.at[1, tiles], 9, 14 + i, z_peer, d)
+
+    def forward(i):
+        tiles = pl.ds(PART * i, PART)
+        arrived(gathered.at[1, tiles], 14 + i)
+        remote(gathered.at[1, tiles], gathered.at[2, tiles], 11, 17 + i, partner, d)
 
     total = jnp.zeros((M, M), F32)
     for i in range(0, TILES, 2):
@@ -401,6 +429,7 @@
         remote(part.at[to], rs_buf.at[mine], 4, 4, lax.rem(to, 4), y_pos * 8 + (to // 4) * 4 + x_pos)
     rs_buf[mine] = part[mine]
     arrived(rs_buf.at[pl.ds(0, 7)], 4)
+    exchange(0)
     acc = rs_buf[0]
     for i in range(1, 8):
         acc = acc + rs_buf[i]
@@ -421,6 +450,8 @@
         remote(gsum.at[mine], gsum.at[mine], 6, 6, lax.rem(to, 4), y_pos * 8 + (to // 4) * 4 + x_pos)
     arrived(gsum.at[pl.ds(0, 7)], 6)
 
+    exchange(1)
+    remote(own.at[pl.ds(0, EARLY)], gathered.at[0, pl.ds(0, EARLY)], 10, 16, partner, d)
     for i in range(8):
         packed[24 * i:24 * i + 24] = gsum[i]
     work[0:64, 0:128] = packed[0:64]
@@ -431,30 +462,60 @@
     work[128:192, 128:256] = pltpu.roll(packed[128:192], 64, 1)
     invert_factor(work, inv_ref)
 
+    def place(tile):
+        return tile // 18, pl.ds(pl.multiple_of(128 * lax.rem(tile, 18), 128), 128)
+
+    def product(rows, block, n):
+        columns = jnp.concatenate([block[2 * n], block[2 * n + 1]], 1)
+        return jnp.dot(rows, columns, precision=lax.Precision.HIGHEST, preferred_element_type=F32)
+
     def rotate(n, c):
-        columns = jnp.concatenate([own[2 * n], own[2 * n + 1]], 1)
-        product = jnp.dot(inv_ref[:, 0:M], columns, precision=lax.Precision.HIGHEST, preferred_element_type=F32)
+        result = product(inv_ref[:, 0:M], own, EARLY // 2 + n)
         for i in range(2):
-            tile = quarter(b) + 2 * n + i
-            place = out_ref.at[tile // 18, :, pl.ds(pl.multiple_of(128 * lax.rem(tile, 18), 128), 128)]
+            plane, lanes = place(quarter(b) + EARLY + 2 * n + i)
             for band in range(4):
-                rot[2 * n + i, band] = product[48 * band:48 * band + 48, 128 * i:128 * i + 128]
-
-            @pl.when(jnp.logical_or(b < 2, 2 * n + i > 0))
-            def _():
-                for away in (2, 3, 1):
-                    to = lax.rem(b + away, 4)
-                    remote(rot.at[2 * n + i, to], place, 8, 7 + b, to, d)
-                local(rot.at[2 * n + i, b], place, 7 + b)
+                rot[2 * n + i, band] = result[48 * band:48 * band + 48, 128 * i:128 * i + 128]
+            for away in (2, 3, 1):
+                to = lax.rem(b + away, 4)
+                remote(rot.at[2 * n + i, to], out_ref.at[plane, :, lanes], 8, 7 + b, to, d)
+            local(rot.at[2 * n + i, b], out_ref.at[plane, :, lanes], 7 + b)
         return c
 
-    lax.fori_loop(0, TILES // 2, rotate, 0)
-
-    tile = rot.at[0, 0]
-    mine_tiles = jnp.where(b < 2, 14, 13)
+    def rotate_early(block, band):
+        def body(n, c):
+            result = product(inv_ref[pl.ds(pl.multiple_of(48 * b, 8), 48), 0:M], block, n)
+            for i in range(2):
+                plane, lanes = place(quarter(band) + 2 * n + i)
+
+                def keep():
+                    out_ref[plane, :, lanes] = result[:, 128 * i:128 * i + 128]
+
+                if i == 0:
+                    pl.when(jnp.logical_or(band < 2, n > 0))(keep)
+                else:
+                    keep()
+            return c
+
+        lax.fori_loop(0, EARLY // 2, body, 0)
+
+    lax.fori_loop(0, (TILES - EARLY) // 2, rotate, 0)
+    forward(0)
+    forward(1)
+    rotate_early(own, b)
+    arrived(gathered.at[0, pl.ds(0, EARLY)], 16)
+    rotate_early(gathered.at[0], partner)
+    rotate_early(gathered.at[1], z_peer)
+    for i in range(2):
+        arrived(gathered.at[2, pl.ds(PART * i, PART)], 17 + i)
+    rotate_early(gathered.at[2], other)
+
+    late = TILES - EARLY
     for band in range(4):
-        arrived(rot.at[pl.ds(0, 14 if band < 2 else 13), 0], 7 + band)
-    drain(tile, send_sems.at[8], 3 * mine_tiles)
+        arrived(rot.at[pl.ds(0, late), 0], 7 + band)
+    drain(rot.at[0, 0], send_sems.at[8], 3 * late)
+    drain(gathered.at[0, pl.ds(0, PART)], send_sems.at[9], 2)
+    drain(gathered.at[0, pl.ds(0, EARLY)], send_sems.at[10], 1)
+    drain(gathered.at[0, pl.ds(0, PART)], send_sems.at[11], 2)
     orbital = recv.at[0, 0, :, 0, :]
     drain(orbital, send_sems.at[0], jnp.where(two, 46, 47))
     drain(half_dst, send_sems.at[1], 31)
@@ -478,8 +539,8 @@
             pltpu.VMEM((2, 4, 3, 8, 1152), F32),
             pltpu.VMEM((256, 256), BF16),
             pltpu.VMEM((192, 192), BF16),
-            pltpu.VMEM((36, 96, 128), F32),
-            pltpu.VMEM((36, 96, 128), F32),
+            pltpu.VMEM((48, 96, 128), F32),
+            pltpu.VMEM((48, 96, 128), F32),
             pltpu.VMEM((24, 96, 128), F32),
             pltpu.VMEM((2, 4, 54, 8, 128), F32),
             pltpu.VMEM((TILES, M, 128), F32),
@@ -491,9 +552,11 @@
             pltpu.VMEM((M, 128), F32),
             pltpu.VMEM((M, 256), F32),
             pltpu.VMEM((M, 256), F32),
-            pltpu.VMEM((TILES, 4, 48, 128), F32),
-            pltpu.SemaphoreType.DMA((9,)),
-            pltpu.SemaphoreType.DMA((14,)),
+            pltpu.VMEM((TILES - EARLY, 4, 48, 128), F32),
+            pltpu.VMEM((3, EARLY, M, 128), F32),
+            pltpu.SemaphoreType.DMA((12,)),
+            pltpu.SemaphoreType.DMA((20,)),
+            pltpu.SemaphoreType.REGULAR,
         ],
         compiler_params=pltpu.CompilerParams(
             collective_id=0, has_side_effects=True, vmem_limit_bytes=56 * 2**20),

time: 114 us -> 107 us (0.939)
  Pallas kernels: 111 us -> 104 us
    pallas_call x1, Pallas kernels: 111 us -> 104 us  [per_device(): pl.pallas_call(kernel, out_shape=jax.ShapeDtypeStruct((3, 48, 2304), F32)...]
where the time goes in v4:
time: 107 us
  Pallas kernels  104 us (97%)
  local copies, waits for them, and re-layouts  2.47 us (2%)
    pallas_call x1, Pallas kernels, per_device(): pl.pallas_call(kernel, out_shape=jax.ShapeDtypeStruct((3, 48, 2304), F32)...  104 us
    unnamed x1, local copies, waits for them, and re-layouts  2.47 us

profile of v4, /device:TPU:1, one launch (start us, length us, event | category | flops | bytes accessed | tf_op | source)
XLA Modules:
  0.0 106.6 jit_solution(11394071686215229125)
XLA Ops:
  0.0 104.1 %shard_map.46 = f32[3,48,2304]{2,1,0:T(8,128)} custom-call(f32[3,48,2304]{2,1,0:T(8,128)} %bitcast.3, f32[3,2304]{1,0:T(4,128)} %p_ref.1, bf16[256,256]{1,0:T(8,128)(2,1)} %constant.4.clone.w_hbm, bf16[192,192]{1,0:T(8,128)(2,1)} %constant.5.clone.c_hbm), custom_call_target="tpu_custom_call" | custom-call | tf_op jit(solution)/shard_map/pallas_call | solution.py:532
  104.1 2.5 %copy.6 = f32[48,3,2304]{2,0,1:T(8,128)} copy(f32[48,3,2304]{2,0,1:T(8,128)} %bitcast.2) | data formatting | bytes 2654208

commit v5 on v4

--- a/solution.py
+++ b/solution.py
@@ -270,25 +270,26 @@
     pot[...] = jnp.full(pot.shape, DIAGONAL, F32)
 
     def unpack(load, store):
-        def body(n, c):
-            yb, q = n // 4, lax.rem(n, 4)
-            for j in range(3):
-                rows = to_rows(load(0, yb, q, j), load(1, yb, q, j))
-                for y in range(8):
-                    store(yb * 8 + y, pl.ds(pl.multiple_of(q * 24 + 8 * j, 8), 8), rows[y])
-            return c
-
-        lax.fori_loop(0, 12, body, 0)
+        def body(q, c):
+            for yb in range(3):
+                for j in range(3):
+                    rows = to_rows(load(0, yb, q, j), load(1, yb, q, j))
+                    for y in range(8):
+                        store(yb * 8 + y, pl.ds(pl.multiple_of(q * 24 + 8 * j, 8), 8), rows[y])
+            return c
+
+        lax.fori_loop(0, 4, body, 0)
 
     def chunk(start, t):
-        return pl.ds(pl.multiple_of(start + 128 * t, 128), 128)
+        return pl.ds(start + 128 * t, 128)
 
     def load_potential(side, yb, q, j):
         return [pot_in[side, q, j, :, chunk(yb * 384, t)] for t in range(3)]
 
     def put(field, y, rows, v):
         field[y, rows, :] = v
-        field[24 + y, rows, :] = pltpu.roll(v, 64, 1)
+        if y < 6 or y >= 18:
+            field[24 + y, rows, :] = pltpu.roll(v, 64, 1)
 
     def store_potential(y, rows, v):
         v = SCALE * v
@@ -296,7 +297,7 @@
         put(field_b, y, rows, field_b[y, rows, :] + (0.5 * v) * field_a[y, rows, :])
 
     def step(src, dst, weight):
-        def block(n, c):
+        def block(n):
             y0 = n * ROWS
             values = src[pl.ds(y0, ROWS)].reshape(ROWS * 96, 128)
             high = values.astype(BF16)
@@ -308,7 +309,7 @@
                 columns = jnp.concatenate([jnp.concatenate([high[one], high[other]], 1),
                                            jnp.concatenate([low[one], low[other]], 1)], 0)
                 along_x.append(jnp.dot(c_ref[...], columns, preferred_element_type=F32))
-            at = [lax.rem(y0 + 48 + s, 48) for s in range(-6, ROWS + 6)]
+            at = [(y0 + s) % 48 for s in range(-6, ROWS + 6)]
             for i in range(12):
                 rows = pl.ds(8 * i, 8)
                 near = [src[y, rows, :] for y in at]
@@ -322,24 +323,37 @@
                          + along_x[r // 2][96 + 8 * i:96 + 8 * i + 8, half_lanes])
                     acc = acc + ((z[:, :128] + z[:, 128:]) + x)
                     put(dst, y0 + r, rows, weight * acc - dst[y0 + r, rows, :])
-            return c
-
-        lax.fori_loop(0, 24 // ROWS, block, 0)
+
+        for n in range(24 // ROWS):
+            block(n)
 
     def quarter(band):
         return 14 * band - jnp.maximum(band - 1, 0)
 
     def spread(slot):
+        def share(to_b, to_d):
+            begin = 14 * to_b - max(to_b - 1, 0)
+            return (pack.at[slot, lax.rem(to_d, 4), pl.ds(begin, TILES), to_d // 4, :],
+                    own.at[:, 48 * b + first + slot, :])
+
         def send(i, c):
-            to = lax.rem(me + i, 128)
-            to_b, to_d = lax.rem(to, 4), to // 4
-            src = pack.at[slot, lax.rem(to_d, 4), pl.ds(quarter(to_b), TILES), to_d // 4, :]
-            remote(src, own.at[:, 48 * b + first + slot, :], 2, 3, to_b, to_d)
-            return c
-
-        lax.fori_loop(1, 128, send, 0)
-        local(pack.at[slot, lax.rem(d, 4), pl.ds(quarter(b), TILES), d // 4, :],
-              own.at[:, 48 * b + first + slot, :], 3)
+            to_d = lax.rem(d + i, 32)
+            for to_b in range(4):
+                src, dst = share(to_b, to_d)
+                remote(src, dst, 2, 3, to_b, to_d)
+            return c
+
+        lax.fori_loop(1, 32, send, 0)
+        for to_b in range(4):
+            src, dst = share(to_b, d)
+
+            @pl.when(to_b == b)
+            def _():
+                local(src, dst, 3)
+
+            @pl.when(to_b != b)
+            def _():
+                remote(src, dst, 2, 3, to_b, d)
 
     def add_potential():
         arrived(pot_in.at[core], 2)
@@ -358,14 +372,14 @@
             put(field_a, y, rows, v)
             field_b[y, rows, :] = jnp.zeros_like(v)
 
-        def repack(n, c):
-            yb, q = n // 4, lax.rem(n, 4)
-            for j in range(3):
-                rows = [field_a[yb * 8 + y, pl.ds(pl.multiple_of(q * 24 + 8 * j, 8), 8), :] for y in range(8)]
-                left, right = to_tiles(rows)
-                for t in range(3):
-                    pack[slot, q, j * 18 + yb * 3 + t] = left[t]
-                    pack[slot, q, j * 18 + 9 + yb * 3 + t] = right[t]
+        def repack(q, c):
+            for yb in range(3):
+                for j in range(3):
+                    rows = [field_a[yb * 8 + y, pl.ds(pl.multiple_of(q * 24 + 8 * j, 8), 8), :] for y in range(8)]
+                    left, right = to_tiles(rows)
+                    for t in range(3):
+                        pack[slot, q, j * 18 + yb * 3 + t] = left[t]
+                        pack[slot, q, j * 18 + 9 + yb * 3 + t] = right[t]
             return c
 
         arrived(recv.at[slot], slot)
@@ -384,7 +398,7 @@
         def _():
             pl.semaphore_wait(ready, 31)
 
-        lax.fori_loop(0, 12, repack, 0)
+        lax.fori_loop(0, 4, repack, 0)
         spread(slot)
         return c
 

time: 107 us -> 97.2 us (0.908)
  Pallas kernels: 104 us -> 94.4 us
    pallas_call x1, Pallas kernels: 104 us -> 94.4 us  [per_device(): pl.pallas_call(kernel, out_shape=jax.ShapeDtypeStruct((3, 48, 2304), F32)...]
where the time goes in v5:
time: 97.2 us; the launch traced here: 96.9 us
  Pallas kernels  94.4 us (97%)
  local copies, waits for them, and re-layouts  2.47 us (3%)
    pallas_call x1, Pallas kernels, per_device(): pl.pallas_call(kernel, out_shape=jax.ShapeDtypeStruct((3, 48, 2304), F32)...  94.4 us
    unnamed x1, local copies, waits for them, and re-layouts  2.47 us

profile of v5, /device:TPU:1, one launch (start us, length us, event | category | flops | bytes accessed | tf_op | source)
XLA Modules:
  0.0 96.9 jit_solution(10805084612994386825)
XLA Ops:
  0.0 94.4 %shard_map.46 = f32[3,48,2304]{2,1,0:T(8,128)} custom-call(f32[3,48,2304]{2,1,0:T(8,128)} %bitcast.3, f32[3,2304]{1,0:T(4,128)} %p_ref.1, bf16[256,256]{1,0:T(8,128)(2,1)} %constant.4.clone.w_hbm, bf16[192,192]{1,0:T(8,128)(2,1)} %constant.5.clone.c_hbm), custom_call_target="tpu_custom_call" | custom-call | tf_op jit(solution)/shard_map/pallas_call | solution.py:546
  94.4 2.5 %copy.6 = f32[48,3,2304]{2,0,1:T(8,128)} copy(f32[48,3,2304]{2,0,1:T(8,128)} %bitcast.2) | data formatting | bytes 2654208

commit v6 on v5

--- a/solution.py
+++ b/solution.py
@@ -24,7 +24,7 @@
 COEFS = [-0.5 * SCALE * w for w in stencil_weights]
 DIAGONAL = 3.0 * COEFS[0] - 7.0 * SCALE
 TILES = 14
-EARLY = 8
+EARLY = 6
 ROWS = 8
 
 
@@ -113,18 +113,20 @@
     return parts
 
 
-def invert_factor(r, out):
+def invert_factor(r, out, wide):
     lane = lax.broadcasted_iota(jnp.int32, (8, 128), 1)
     sub = lax.broadcasted_iota(jnp.int32, (8, 128), 0)
-    splat = lambda v, i, j: jnp.broadcast_to(v[i:i + 1, j:j + 1], (8, 128))
     spread = lambda v, i: jnp.broadcast_to(v[i:i + 1], (8, 128))
 
     def body(first_row, k):
-        rows = pl.ds(pl.multiple_of(8 * k, 8), 8)
+        rows = pl.ds(8 * k, 8)
         top = [r[rows, 0:128], r[rows, 128:256]]
-        off = 8 * lax.rem(k, 16)
-        block = pltpu.roll(jnp.where(k >= 16, top[1], top[0]), lax.rem(128 - off, 128), 1)
-        s = {(i, j): splat(block, j, i) for i in range(8) for j in range(i + 1)}
+        base = 64 * (k % 2)
+        for i in range(8):
+            at = 8 * (k % 16) + i
+            wide[base + 8 * i:base + 8 * i + 8, :] = jnp.broadcast_to(top[k // 16][:, at:at + 1], (8, 128))
+        s = {(i, j): jnp.broadcast_to(wide[base + 8 * i + j:base + 8 * i + j + 1, :], (8, 128))
+             for i in range(8) for j in range(i + 1)}
         recip, low = [], {}
         for col in range(8):
             recip.append(1.0 / s[col, col])
@@ -171,6 +173,8 @@
         z, w = three_terms(jnp.concatenate(zs, 1)), three_terms(jnp.concatenate(ss, 1))
         left = jnp.concatenate([w[0], w[0], w[1], w[0], w[1], w[2]], 0).astype(BF16)
         right = jnp.concatenate([z[0], z[1], z[0], z[2], z[1], z[0]], 0).astype(BF16)
+        if first_row == 24:
+            return
         live = slice(8 * first_row, M)
         update = lax.dot_general(left[:, live], right, (((0,), (0,)), ((), ())),
                                  preferred_element_type=F32)
@@ -178,15 +182,12 @@
         inside = jnp.logical_and(local >= 0, local < 8)
         r[live, :] = jnp.where(inside, 0.0, r[live, :]) - update
 
-    for part in range(3):
-        def segment(k, c):
-            body(8 * part, k)
-            return c
-        lax.fori_loop(8 * part, 8 * part + 8, segment, 0)
+    for k in range(24):
+        body(k + 1, k)
 
 
 def kernel(x_ref, p_ref, w_hbm, c_hbm, out_ref, recv, pot_in, w_ref, c_ref, field_a, field_b, pot, pack,
-           own, part, rs_buf, xy_buf, sums, gsum, packed, work, inv_ref, rot, gathered, send_sems, recv_sems, ready):
+           own, part, rs_buf, xy_buf, sums, gsum, packed, work, inv_ref, wide, rot, gathered, send_sems, recv_sems, ready):
     b = lax.axis_index("band")
     d = lax.axis_index("dom")
     core = lax.rem(b, 2)
@@ -474,7 +475,7 @@
     work[64:128, 128:256] = packed[128:192]
     work[128:192, 0:128] = packed[128:192]
     work[128:192, 128:256] = pltpu.roll(packed[128:192], 64, 1)
-    invert_factor(work, inv_ref)
+    invert_factor(work, inv_ref, wide)
 
     def place(tile):
         return tile // 18, pl.ds(pl.multiple_of(128 * lax.rem(tile, 18), 128), 128)
@@ -566,6 +567,7 @@
             pltpu.VMEM((M, 128), F32),
             pltpu.VMEM((M, 256), F32),
             pltpu.VMEM((M, 256), F32),
+            pltpu.VMEM((128, 128), F32),
             pltpu.VMEM((TILES - EARLY, 4, 48, 128), F32),
             pltpu.VMEM((3, EARLY, M, 128), F32),
             pltpu.SemaphoreType.DMA((12,)),

time: 97.2 us -> 95.2 us (0.979)
  Pallas kernels: 94.4 us -> 92.6 us
    pallas_call x1, Pallas kernels: 94.4 us -> 92.6 us  [per_device(): pl.pallas_call(kernel, out_shape=jax.ShapeDtypeStruct((3, 48, 2304), F32)...]
where the time goes in v6:
time: 95.2 us; the launch traced here: 95.1 us
  Pallas kernels  92.6 us (97%)
  local copies, waits for them, and re-layouts  2.47 us (3%)
    pallas_call x1, Pallas kernels, per_device(): pl.pallas_call(kernel, out_shape=jax.ShapeDtypeStruct((3, 48, 2304), F32)...  92.6 us
    unnamed x1, local copies, waits for them, and re-layouts  2.47 us

profile of v6, /device:TPU:1, one launch (start us, length us, event | category | flops | bytes accessed | tf_op | source)
XLA Modules:
  0.0 95.1 jit_solution(7308438646165079315)
XLA Ops:
  0.0 92.6 %shard_map.46 = f32[3,48,2304]{2,1,0:T(8,128)} custom-call(f32[3,48,2304]{2,1,0:T(8,128)} %bitcast.3, f32[3,2304]{1,0:T(4,128)} %p_ref.1, bf16[256,256]{1,0:T(8,128)(2,1)} %constant.4.clone.w_hbm, bf16[192,192]{1,0:T(8,128)(2,1)} %constant.5.clone.c_hbm), custom_call_target="tpu_custom_call" | custom-call | tf_op jit(solution)/shard_map/pallas_call | solution.py:547
  92.6 2.5 %copy.6 = f32[48,3,2304]{2,0,1:T(8,128)} copy(f32[48,3,2304]{2,0,1:T(8,128)} %bitcast.2) | data formatting | bytes 2654208

commit v7 on v6

--- a/solution.py
+++ b/solution.py
@@ -357,13 +357,11 @@
                 remote(src, dst, 2, 3, to_b, d)
 
     def add_potential():
+        send_orbital(1)
         arrived(pot_in.at[core], 2)
         remote(pot_in.at[core], pot_in.at[core], 7, 11, partner, d)
         arrived(pot_in.at[core], 11)
         unpack(load_potential, store_potential)
-
-    def send_second():
-        send_orbital(1)
 
     def filter_orbital(slot, c):
         def load(side, yb, q, j):
@@ -384,7 +382,6 @@
             return c
 
         arrived(recv.at[slot], slot)
-        pl.when(slot == 0)(send_second)
         unpack(load, store)
 
         def steps(t, c):

time: 95.2 us -> 94.5 us (level)
  no operation moved by 1% of the time
where the time goes in v7:
time: 94.5 us; the launch traced here: 94.4 us
  Pallas kernels  91.9 us (97%)
  local copies, waits for them, and re-layouts  2.47 us (3%)
    pallas_call x1, Pallas kernels, per_device(): pl.pallas_call(kernel, out_shape=jax.ShapeDtypeStruct((3, 48, 2304), F32)...  91.9 us
    unnamed x1, local copies, waits for them, and re-layouts  2.47 us

profile of v7, /device:TPU:1, one launch (start us, length us, event | category | flops | bytes accessed | tf_op | source)
XLA Modules:
  0.0 94.4 jit_solution(15603670026253939727)
XLA Ops:
  0.0 91.9 %shard_map.46 = f32[3,48,2304]{2,1,0:T(8,128)} custom-call(f32[3,48,2304]{2,1,0:T(8,128)} %bitcast.3, f32[3,2304]{1,0:T(4,128)} %p_ref.1, bf16[256,256]{1,0:T(8,128)(2,1)} %constant.4.clone.w_hbm, bf16[192,192]{1,0:T(8,128)(2,1)} %constant.5.clone.c_hbm), custom_call_target="tpu_custom_call" | custom-call | tf_op jit(solution)/shard_map/pallas_call | solution.py:544
  91.9 2.5 %copy.6 = f32[48,3,2304]{2,0,1:T(8,128)} copy(f32[48,3,2304]{2,0,1:T(8,128)} %bitcast.2) | data formatting | bytes 2654208
